TPU v7x, 768 devices: a whole 4x8x12 slice. The times are simulated.
768 devices in a mesh: row: 32 (over z_hi, y), col: 24 (over x, z_lo, core).
Axes of the slice: x: 4, y: 8, z: 12 (z_hi: 4, z_lo: 3; z = z_hi * 3 + z_lo), core: 2. Of those that a mesh axis runs over, the one named last changes fastest.
Arguments:
- features: bfloat16 [24, 4096, 128], P('col', 'row'), may hold values from -6 to 6
- out_degree: int32 [24, 4096], P('col', 'row'), may hold values from 8 to 96
- in_degree: int32 [32, 3072], P('row', 'col'), may hold values from 8 to 96
- tile_pos: int32 [32, 24, 32, 2], P('row', 'col'), may hold values from 0 to 15, as said below
- tile_count: int32 [32, 24], P('row', 'col'), may hold values from 1 to 32, as said below
- tiles: bfloat16 [32, 24, 32, 256, 256], P('row', 'col'), as said below
- weight: bfloat16 [128, 256], replicated, may hold values from -0.5 to 0.5
- cotangent: bfloat16 [32, 3072, 256], P('row', 'col'), may hold values from -0.076171875 to 0.076171875
Outputs:
- output: bfloat16 [32, 3072, 256], P('row', 'col')
- grad_weight: float32 [128, 256], replicated
Inputs may be any that keep to these rules, and one draw needn't show every extreme that they name: `tile_pos`: each device's slots hold distinct tile positions of its block of 3072 x 4096 nodes, row tile first; slots from tile_count on hold positions too and are not used; some device's first slot is the block's last tile. `tile_count`: some device uses all 32 slots. `tiles`: nonnegative edge weights, zero where there is no edge; most entries of a tile are zero.
All inputs are finite; a program needn't handle non-finite values.
Results may differ from a plain program's by a relative error of at most 0.025.
Values may be sent and summed in bfloat16 or wider, within the bound.
No kernel may reach another device: no remote copies, remote signals or barrier semaphores. Data moves between devices by JAX's collectives and lax.ppermute only.
A program may use at most 32 MiB of HBM per device.

v0:
```python
import jax
import jax.numpy as jnp
from jax import lax
from jax.sharding import PartitionSpec as P


def per_device(features, out_degree, in_degree, tile_pos, tile_count, tiles, weight, cotangent):
    node_dev = features.shape[1]
    channels = features.shape[2]
    tile_side = tiles.shape[3]
    row_tiles = lax.axis_size("col") * node_dev // tile_side
    scaled = (
        features[0].astype(jnp.float32) * lax.rsqrt(out_degree[0].astype(jnp.float32))[:, None]
    ).astype(jnp.bfloat16)
    gathered = lax.all_gather(scaled, "row", axis=0, tiled=True)
    blocks = gathered.reshape(-1, tile_side, channels)
    positions = tile_pos[0, 0]
    live_count = tile_count[0, 0]
    tile_block = tiles[0, 0]
    picked = blocks[positions[:, 1]]
    product = jnp.einsum("tij,tjk->tik", tile_block, picked, preferred_element_type=jnp.float32)
    live = jnp.arange(tile_block.shape[0]) < live_count
    row_ids = jnp.arange(row_tiles)
    select = ((positions[:, 0][None, :] == row_ids[:, None]) & live[None, :]).astype(jnp.float32)
    partial_value = jnp.einsum(
        "rt,tik->rik", select, product, precision=lax.Precision.HIGHEST
    ).reshape(-1, channels)
    summed = lax.psum(partial_value.astype(jnp.bfloat16), "col").astype(jnp.float32)
    own_sum = lax.dynamic_slice_in_dim(summed, lax.axis_index("col") * node_dev, node_dev, 0)
    aggregated = (own_sum * lax.rsqrt(in_degree[0].astype(jnp.float32))[:, None]).astype(
        jnp.bfloat16
    )
    output = jnp.dot(aggregated, weight, preferred_element_type=jnp.float32).astype(jnp.bfloat16)[
        None
    ]
    local_grad = lax.dot_general(
        aggregated, cotangent[0], (((0,), (0,)), ((), ())), preferred_element_type=jnp.float32
    )
    grad_weight = lax.psum(local_grad, ("row", "col"))
    return (output, grad_weight)


def solution(mesh):
    return jax.shard_map(
        per_device,
        mesh=mesh,
        in_specs=(
            P("col", "row", None),
            P("col", "row"),
            P("row", "col"),
            P("row", "col", None, None),
            P("row", "col"),
            P("row", "col", None, None, None),
            P(),
            P("row", "col", None),
        ),
        out_specs=(P("row", "col", None), P()),
        check_vma=False,
    )
```

profile of v0, /device:TPU:1, one launch (start us, length us, event | category | flops | bytes accessed | tf_op | source)
XLA Modules:
  0.0 828.6 jit_solution(2231954624841197690)
XLA Ops:
  7.2 0.0 copy-start
  7.2 0.0 all-gather.2.cloned.1.call-start
  7.2 0.7 rsqrt_bitcast_fusion.1
  7.9 1.5 fusion.8
  9.3 0.0 all-gather.2.cloned.1.call-update
  9.4 0.0 all-reduce.3.cloned.1.call-start
  10.1 0.8 slice_bitcast_fusion
  10.9 97.7 %all-gather.2.cloned.1.call-done = bf16[4096,128]{1,0:T(8,128)(2,1)} async-done(((bf16[128,128]{1,0:T(8,128)(2,1)}), bf16[4096,128]{1,0:T(8,128)(2,1)}) %all-gather.2.cloned.1.call-update) | async-done | bytes 1048592 | tf_op jit(solution)/shard_map/all_gather | solution.py:15
  108.6 2.2 gather_fusion
  110.7 5.6 fusion.2
  116.4 5.5 copy.11
  121.9 3.8 fusion.4
  125.7 1.1 copy.10
  126.8 0.0 all-reduce.3.cloned.1.call-update
  126.9 0.0 all-reduce.5.cloned.1.call-start
  126.9 0.0 copy-done.2
  127.0 217.7 %all-reduce.3.cloned.1.call-done = bf16[3072,128]{1,0:T(8,128)(2,1)} async-done(((bf16[3072,128]{1,0:T(8,128)(2,1)}), bf16[3072,128]{1,0:T(8,128)(2,1)}) %all-reduce.3.cloned.1.call-update) | async-done | bytes 786448 | tf_op jit(solution)/shard_map/psum | solution.py:28
  344.7 0.0 copy-done
  344.7 1.7 fusion.9
  346.4 0.0 all-reduce.5.cloned.1.call-update
  346.4 0.0 copy-done.1
  346.4 1.6 fusion.7
  348.0 472.5 %all-reduce.5.cloned.1.call-done = f32[128,256]{1,0:T(8,128)} async-done(((f32[128,256]{1,0:T(8,128)}), f32[128,256]{1,0:T(8,128)}) %all-reduce.5.cloned.1.call-update) | async-done | bytes 131088 | tf_op jit(solution)/shard_map/psum | solution.py:39
  820.5 1.6 copy.15
  (5 shorter events, 0.0 us)
Async XLA Ops:
  7.2 337.5 %copy-start = (bf16[1,128,256]{2,1,0:T(8,128)(2,1)S(1)}, bf16[1,128,256]{2,1,0:T(8,128)(2,1)}, u32[]{:S(2)}) copy-start(bf16[1,128,256]{2,1,0:T(8,128)(2,1)} %param.15) | copy-start | bytes 196612
  7.2 101.4 %all-gather.2.cloned.1.call-start = ((), (), s32[]{:S(2)}) async-start(), calls=%async_computation | async-start | bytes 1081344 | tf_op jit(solution)/shard_map/all_gather | solution.py:15
  9.4 335.3 %all-reduce.3.cloned.1.call-start = ((), (), s32[]{:S(2)}) async-start(), calls=%async_computation.1 | async-start | bytes 1572864 | tf_op jit(solution)/shard_map/psum | solution.py:28
  121.9 5.0 copy-start.2
  121.9 224.5 %copy-start.1 = (bf16[128,256]{1,0:T(8,128)(2,1)S(1)}, bf16[128,256]{1,0:T(8,128)(2,1)}, u32[]{:S(2)}) copy-start(bf16[128,256]{1,0:T(8,128)(2,1)} %param.14) | copy-start | bytes 196612
  126.9 693.7 %all-reduce.5.cloned.1.call-start = ((), (), s32[]{:S(2)}) async-start(), calls=%async_computation.2 | async-start | bytes 262144 | tf_op jit(solution)/shard_map/psum | solution.py:39
Sparse Core Ops, SparseCore 0:
  12.3 96.1 all-gather.1
  127.0 217.6 all-reduce.2
  351.5 468.9 all-reduce.4
where the time goes:
time: 830 us; the launch traced here: 829 us
  waiting for transfers between devices  788 us (95%)
  between operations  14.5 us (2%)
  matrix products  12.8 us (2%)
  local copies, waits for them, and re-layouts  10.4 us (1%)
    psum x1, waiting for transfers between devices, per_device(): grad_weight = lax.psum(local_grad, ('row', 'col'))  473 us
    psum x1, waiting for transfers between devices, per_device(): lax.psum(partial_value.astype(jnp.bfloat16), 'col').astype(jnp.float32)  218 us
    all_gather x1, waiting for transfers between devices, per_device(): gathered = lax.all_gather(scaled, 'row', axis=0, tiled=True)  97.7 us
  transfers between devices with their start and end apart: 3, of which 3 were waited for; matrix products, arithmetic and copies ran while one was open for 0% of the time, Pallas kernels for 0%

commit v1 on v0

v1 whole, which is shorter than its diff:
```python
import jax
import jax.numpy as jnp
from jax import lax
from jax.experimental import pallas as pl
from jax.experimental.pallas import tpu as pltpu
from jax.sharding import Mesh, PartitionSpec as P

Z_HI, Y, X, Z_LO, CORE = 4, 8, 4, 3, 2
ROW = ("zh", "y")
COL = ("x", "zl", "core")
NODE = 128
TILE = 256
CH = 128
F = 256
ROW_TILES = X * Z_LO
N_COL = X * Z_LO * CORE
N_ROW = Z_HI * Y
PIECE = 11
UNROLL = 4


def tile_kernel(pos_ref, count_ref, core_ref, tiles_ref, source_ref, keep_ref, send_ref, acc_ref):
    count = count_ref[0]
    core = core_ref[0]
    slots = tiles_ref.shape[0]
    acc_ref[...] = jnp.zeros_like(acc_ref)

    def chunk(k, carry):
        products = []
        for u in range(UNROLL):
            s = k * UNROLL + u
            j = pos_ref[1, s]
            picked = source_ref[pl.ds(2 * (j % (Y // 2)), 2), j // (Y // 2)].reshape(TILE, CH)
            picked = jnp.where(s < count, picked, jnp.zeros_like(picked))
            products.append(jnp.dot(tiles_ref[s], picked, preferred_element_type=jnp.float32))
        for u in range(UNROLL):
            i = pos_ref[0, k * UNROLL + u]
            acc_ref[i] += products[u].reshape(CORE, NODE, CH)
        return carry

    lax.fori_loop(0, (count + UNROLL - 1) // UNROLL, chunk, 0)
    keep_ref[...] = acc_ref[:, core]
    send_ref[...] = acc_ref[:, 1 - core].astype(jnp.bfloat16)


def tile_product(positions, count, core, tiles, source):
    smem = pl.BlockSpec(memory_space=pltpu.SMEM)
    vmem = pl.BlockSpec(memory_space=pltpu.VMEM)
    return pl.pallas_call(
        tile_kernel,
        out_shape=(
            jax.ShapeDtypeStruct((ROW_TILES, NODE, CH), jnp.float32),
            jax.ShapeDtypeStruct((ROW_TILES, NODE, CH), jnp.bfloat16),
        ),
        in_specs=[smem, smem, smem, vmem, vmem],
        out_specs=(vmem, vmem),
        scratch_shapes=[pltpu.VMEM((ROW_TILES, CORE, NODE, CH), jnp.float32)],
        compiler_params=pltpu.CompilerParams(vmem_limit_bytes=32 * 1024 * 1024),
        cost_estimate=pl.CostEstimate(
            flops=2 * 32 * TILE * TILE * CH, bytes_accessed=8 * 1024 * 1024, transcendentals=0
        ),
        name="tile_product",
    )(positions, count, core, tiles, source)


def node_kernel(parts_ref, degree_ref, weight_ref, cot_ref, out_ref, grad_ref):
    total = jnp.sum(parts_ref[...].astype(jnp.float32), axis=0)
    aggregated = (total * lax.rsqrt(degree_ref[...].astype(jnp.float32))).astype(jnp.bfloat16)
    out_ref[...] = jnp.dot(
        aggregated, weight_ref[...], preferred_element_type=jnp.float32
    ).astype(jnp.bfloat16)
    grad = lax.dot_general(
        aggregated, cot_ref[...], (((0,), (0,)), ((), ())), preferred_element_type=jnp.float32
    )
    grad_ref[:CH] = grad[:, :CH]
    grad_ref[CH : 2 * CH] = grad[:, CH:]
    grad_ref[2 * CH :] = jnp.zeros_like(grad_ref[2 * CH :])


def node_stage(parts, degree, weight, cotangent):
    vmem = pl.BlockSpec(memory_space=pltpu.VMEM)
    return pl.pallas_call(
        node_kernel,
        out_shape=(
            jax.ShapeDtypeStruct((NODE, F), jnp.bfloat16),
            jax.ShapeDtypeStruct((N_COL * PIECE, CH), jnp.float32),
        ),
        in_specs=[vmem] * 4,
        out_specs=(vmem, vmem),
        name="node_stage",
    )(parts, degree, weight, cotangent)


def exchange(parts, axes):
    return lax.all_to_all(parts, axes, 0, 0)


def spread(piece, axes, n):
    return exchange(jnp.broadcast_to(piece[None], (n,) + piece.shape), axes)


def per_device(features, out_degree, in_degree, tile_pos, tile_count, tiles, weight, cotangent):
    core = lax.axis_index("core")
    scaled = (
        features[0].astype(jnp.float32) * lax.rsqrt(out_degree[0].astype(jnp.float32))[:, None]
    ).astype(jnp.bfloat16)
    over_z = lax.all_gather(scaled, "zh", axis=0)
    source = spread(over_z, "y", Y)

    keep, send = tile_product(
        tile_pos[0, 0].T, tile_count[0], core.reshape(1), tiles[0, 0], source
    )
    arrived = lax.ppermute(send, "core", [(0, 1), (1, 0)])
    pair = (keep + arrived.astype(jnp.float32)).astype(jnp.bfloat16)
    parts = exchange(pair, ("x", "zl"))

    output, local_grad = node_stage(parts, in_degree[0][:, None], weight, cotangent[0])

    piece = jnp.sum(exchange(local_grad.reshape(N_COL, PIECE, CH), COL), axis=0)
    piece = jnp.sum(spread(piece, ROW, N_ROW), axis=0)
    grad = spread(piece, COL, N_COL).reshape(N_COL * PIECE, CH)
    grad_weight = jnp.concatenate([grad[:CH], grad[CH : 2 * CH]], axis=1)
    return (output[None], grad_weight)


def solution(mesh):
    fine = Mesh(mesh.devices.reshape(Z_HI, Y, X, Z_LO, CORE), ROW + COL)
    return jax.shard_map(
        per_device,
        mesh=fine,
        in_specs=(
            P(COL, ROW, None),
            P(COL, ROW),
            P(ROW, COL),
            P(ROW, COL, None, None),
            P(ROW, COL),
            P(ROW, COL, None, None, None),
            P(),
            P(ROW, COL, None),
        ),
        out_specs=(P(ROW, COL, None), P()),
        check_vma=False,
    )
```

time: 830 us -> 145 us (0.17)
  waiting for transfers between devices: 788 us -> 36.5 us
  blocking collectives: 0 us -> 75.2 us
  starting transfers between devices: 0.12 us -> 17.3 us
  between operations: 14.5 us -> 1.37 us
  matrix products: 12.8 us -> 0 us
    psum x2 -> x0, waiting for transfers between devices: 690 us -> none  [the longest x1 473 us: per_device(): grad_weight = lax.psum(local_grad, ('row', 'col'))]
    all_gather x1 -> x0, waiting for transfers between devices: 97.7 us -> none  [per_device(): gathered = lax.all_gather(scaled, 'row', axis=0, tiled=True)]
    all_to_all x0 -> x3, blocking collectives: none -> 52.1 us  [exchange(): return lax.all_to_all(parts, axes, 0, 0)]
    all_to_all x0 -> x2, waiting for transfers between devices: none -> 35.1 us  [exchange(): return lax.all_to_all(parts, axes, 0, 0)]
    all_gather x0 -> x1, blocking collectives: none -> 23.1 us  [per_device(): over_z = lax.all_gather(scaled, 'zh', axis=0)]
    all_to_all x0 -> x2, starting transfers between devices: none -> 12.8 us  [exchange(): return lax.all_to_all(parts, axes, 0, 0)]
    dot_general x4 -> x0, matrix products: 12.8 us -> none  [the longest x1 5.65 us: per_device(): jnp.einsum('tij,tjk->tik', tile_block, picked, preferred_element_type=jnp...]
  transfers between devices with their start and end apart: 3 -> 3, of which waited for: 3 -> 3; matrix products, arithmetic and copies ran while one was open for 0% -> 1% of each run, Pallas kernels for 0% -> 0%
where the time goes in v1:
time: 145 us; the launch traced here: 144 us
  blocking collectives  75.2 us (52%)
  waiting for transfers between devices  36.5 us (25%)
  starting transfers between devices  17.3 us (12%)
  local copies, waits for them, and re-layouts  6.56 us (5%)
  Pallas kernels  4.28 us (3%)
  other arithmetic  3.1 us (2%)
    all_to_all x3, blocking collectives, exchange(): return lax.all_to_all(parts, axes, 0, 0)  52.1 us
    all_to_all x2, waiting for transfers between devices, exchange(): return lax.all_to_all(parts, axes, 0, 0)  35.1 us
    all_gather x1, blocking collectives, per_device(): over_z = lax.all_gather(scaled, 'zh', axis=0)  23.1 us
    all_to_all x2, starting transfers between devices, exchange(): return lax.all_to_all(parts, axes, 0, 0)  12.8 us
    ppermute x1, starting transfers between devices, per_device(): arrived = lax.ppermute(send, 'core', [(0, 1), (1, 0)])  4.52 us
    unnamed x8, local copies, waits for them, and re-layouts  3.63 us
  transfers between devices with their start and end apart: 3, of which 3 were waited for; matrix products, arithmetic and copies ran while one was open for 1% of the time, Pallas kernels for 0%

profile of v1, /device:TPU:1, one launch (start us, length us, event | category | flops | bytes accessed | tf_op | source)
XLA Modules:
  0.0 144.3 jit_solution(10815337225111575896)
XLA Ops:
  0.6 0.7 rsqrt_bitcast_fusion
  1.3 0.8 multiply_convert_fusion
  2.1 23.1 %all_gather.4 = bf16[4,128,128]{2,1,0:T(8,128)(2,1)S(1)} all-gather(bf16[1,128,128]{2,1,0:T(8,128)(2,1)S(1)} %multiply_convert_fusion), channel_id=1, replica_groups=mesh['zh'=4,'y'=8,'x'=4,'zl'=3,'core'=2] {'zh'}, dimensions={0}, use_global_device_ids=true | all-gather | bytes 163840 | tf_op jit(solution)/shard_map/all_gather | solution.py:107
  25.3 1.2 broadcast_in_dim.8
  26.5 6.8 %all-to-all-start = ((bf16[8,4,128,128]{3,2,1,0:T(8,128)(2,1)}), bf16[8,4,128,128]{3,2,1,0:T(8,128)(2,1)S(1)}, u32[]{:S(2)}, u32[]{:S(2)}) async-start(bf16[8,4,128,128]{3,2,1,0:T(8,128)(2,1)} %broadcast_in_dim.8), calls=%async_computation | async-start | bytes 2097152 | tf_op jit(solution)/shard_map/all_to_all | solution.py:95
  33.3 0.0 copy-start.3
  34.0 26.1 %all-to-all-done.source_ref = bf16[8,4,128,128]{3,2,1,0:T(8,128)(2,1)S(1)} async-done(((bf16[8,4,128,128]{3,2,1,0:T(8,128)(2,1)}), bf16[8,4,128,128]{3,2,1,0:T(8,128)(2,1)S(1)}, u32[]{:S(2)}, u32[]{:S(2)}) %all-to-all-start) | async-done | bytes 1048608 | tf_op jit(solution)/shard_map/all_to_all | solution.py:95
  60.1 2.2 %copy-done = bf16[1,1,32,256,256]{4,3,2,1,0:T(8,128)(2,1)S(1)} copy-done((bf16[1,1,32,256,256]{4,3,2,1,0:T(8,128)(2,1)S(1)}, bf16[1,1,32,256,256]{4,3,2,1,0:T(8,128)(2,1)}, u32[]{:S(2)}) %copy-start) | copy-done | bytes 4194328
  62.3 0.7 copy-done.1
  63.0 2.3 %tile_product.1 = (f32[12,128,128]{2,1,0:T(8,128)S(1)}, bf16[12,128,128]{2,1,0:T(8,128)(2,1)S(1)}) custom-call(s32[2,32]{1,0:T(2,128)S(1)} %bitcast.13, s32[1]{0:T(128)} %bitcast.11.count_ref, s32[1]{0:T(128)} %bitcast.3.core_ref, bf16[32,256,256]{2,1,0:T(8,128)(2,1)S(1)} %bitcast.12, bf16[8,4,128,128]{3,2,1,0:T(8,128)(2,1)S(1)} %all-to-all-done.source_ref), custom_call_target="tpu_custom_call" | custom-call | flops 536870912 | bytes 8388608 | tf_op jit(solution)/shard_map/tile_product/pallas_call | solution.py:49
  65.3 4.5 %collective-permute-start = (bf16[12,128,128]{2,1,0:T(8,128)(2,1)S(1)}, bf16[12,128,128]{2,1,0:T(8,128)(2,1)S(1)}, u32[]{:S(2)}, u32[]{:S(2)}) collective-permute-start(bf16[12,128,128]{2,1,0:T(8,128)(2,1)S(1)} %get-tuple-element.7), channel_id=1, source_target_pairs={{0,1},{1,0},{2,3},{3,2},{4,5},{5,4},{6,7},{7,6},{8,9},{9,8},{10,11... | collective-permute-start | bytes 1179656 | tf_op jit(solution)/shard_map/ppermute | solution.py:113
  69.8 1.3 collective-permute-done
  71.2 0.9 add_convert_fusion
  72.0 5.9 %all-to-all-start.1 = ((bf16[12,128,128]{2,1,0:T(8,128)(2,1)}), bf16[12,128,128]{2,1,0:T(8,128)(2,1)S(1)}, u32[]{:S(2)}, u32[]{:S(2)}) async-start(bf16[12,128,128]{2,1,0:T(8,128)(2,1)} %add_convert_fusion), calls=%async_computation.1 | async-start | bytes 786432 | tf_op jit(solution)/shard_map/all_to_all | solution.py:95
  78.0 0.0 copy-done.3
  78.0 0.7 copy.14.degree_ref
  78.7 9.0 %all-to-all-done.1.parts_ref = bf16[12,128,128]{2,1,0:T(8,128)(2,1)S(1)} async-done(((bf16[12,128,128]{2,1,0:T(8,128)(2,1)}), bf16[12,128,128]{2,1,0:T(8,128)(2,1)S(1)}, u32[]{:S(2)}, u32[]{:S(2)}) %all-to-all-start.1) | async-done | bytes 393248 | tf_op jit(solution)/shard_map/all_to_all | solution.py:95
  87.7 0.8 copy-done.2
  88.5 2.0 %node_stage.1 = (bf16[128,256]{1,0:T(8,128)(2,1)}, f32[264,128]{1,0:T(8,128)}) custom-call(bf16[12,128,128]{2,1,0:T(8,128)(2,1)} %copy-done.2, s32[128,1]{1,0:T(8,128)} %copy.14.degree_ref, bf16[128,256]{1,0:T(8,128)(2,1)} %weight_ref.1, bf16[128,256]{1,0:T(8,128)(2,1)} %bitcast.14), custom_call_target="tpu_custom_call" | custom-call | tf_op jit(solution)/shard_map/node_stage/pallas_call | solution.py:82
  90.4 0.9 reshape.32
  91.4 13.0 %all_to_all.25 = f32[24,11,128]{2,1,0:T(8,128)S(1)} all-to-all(f32[24,11,128]{2,1,0:T(8,128)S(1)} %reshape.32), channel_id=1, replica_groups=mesh['zh'=4,'y'=8,'x'=4,'zl'=3,'core'=2] {'x','zl','core'}, dimensions={0} | all-to-all | bytes 270336 | tf_op jit(solution)/shard_map/all_to_all | solution.py:95
  104.5 24.1 %all_to_all.26 = f32[32,11,128]{2,1,0:T(8,128)S(1)} all-to-all(f32[32,11,128]{2,1,0:T(8,128)S(1)} %broadcast_in_dim.10), channel_id=1, replica_groups=mesh['zh'=4,'y'=8,'x'=4,'zl'=3,'core'=2] {'zh','y'}, dimensions={0} | all-to-all | bytes 360448 | tf_op jit(solution)/shard_map/all_to_all | solution.py:95
  128.6 15.0 %all_to_all.27 = f32[24,11,128]{2,1,0:T(8,128)S(1)} all-to-all(f32[24,11,128]{2,1,0:T(8,128)S(1)} %broadcast_in_dim.11), channel_id=1, replica_groups=mesh['zh'=4,'y'=8,'x'=4,'zl'=3,'core'=2] {'x','zl','core'}, dimensions={0} | all-to-all | bytes 270336 | tf_op jit(solution)/shard_map/all_to_all | solution.py:95
  143.6 0.7 pad_maximum_fusion
  (9 shorter events, 0.1 us)
Async XLA Ops:
  26.5 33.6 %all-to-all-start = ((bf16[8,4,128,128]{3,2,1,0:T(8,128)(2,1)}), bf16[8,4,128,128]{3,2,1,0:T(8,128)(2,1)S(1)}, u32[]{:S(2)}, u32[]{:S(2)}) async-start(bf16[8,4,128,128]{3,2,1,0:T(8,128)(2,1)} %broadcast_in_dim.8), calls=%async_computation | async-start | bytes 2097152 | tf_op jit(solution)/shard_map/all_to_all | solution.py:95
  33.3 44.7 %copy-start.3 = (s32[1,128]{1,0:T(1,128)S(1)}, s32[1,128]{1,0:T(1,128)}, u32[]{:S(2)}) copy-start(s32[1,128]{1,0:T(1,128)} %param.10) | copy-start | bytes 1540
  60.1 2.2 %copy-start = (bf16[1,1,32,256,256]{4,3,2,1,0:T(8,128)(2,1)S(1)}, bf16[1,1,32,256,256]{4,3,2,1,0:T(8,128)(2,1)}, u32[]{:S(2)}) copy-start(bf16[1,1,32,256,256]{4,3,2,1,0:T(8,128)(2,1)} %param.13) | copy-start | bytes 12582916
  62.3 0.7 copy-start.1
  65.3 5.9 %collective-permute-start = (bf16[12,128,128]{2,1,0:T(8,128)(2,1)S(1)}, bf16[12,128,128]{2,1,0:T(8,128)(2,1)S(1)}, u32[]{:S(2)}, u32[]{:S(2)}) collective-permute-start(bf16[12,128,128]{2,1,0:T(8,128)(2,1)S(1)} %get-tuple-element.7), channel_id=1, source_target_pairs={{0,1},{1,0},{2,3},{3,2},{4,5},{5,4},{6,7},{7,6},{8,9},{9,8},{10,11... | collective-permute-start | bytes 1179656 | tf_op jit(solution)/shard_map/ppermute | solution.py:113
  72.0 15.7 %all-to-all-start.1 = ((bf16[12,128,128]{2,1,0:T(8,128)(2,1)}), bf16[12,128,128]{2,1,0:T(8,128)(2,1)S(1)}, u32[]{:S(2)}, u32[]{:S(2)}) async-start(bf16[12,128,128]{2,1,0:T(8,128)(2,1)} %add_convert_fusion), calls=%async_computation.1 | async-start | bytes 786432 | tf_op jit(solution)/shard_map/all_to_all | solution.py:95
  87.7 0.8 copy-start.2

commit v2 on v1

v2 whole, which is shorter than its diff:
```python
import jax
import jax.numpy as jnp
from jax import lax
from jax.experimental import pallas as pl
from jax.experimental.pallas import tpu as pltpu
from jax.sharding import Mesh, PartitionSpec as P

Z_HI, Y, X, Z_LO, CORE = 4, 8, 4, 3, 2
ROW = ("zh", "y")
COL = ("x", "zl", "core")
NODE = 128
TILE = 256
CH = 128
F = 256
ROW_TILES = X * Z_LO
N_ROW = Z_HI * Y
PIECE = 32
UNROLL = 4


def tile_kernel(
    pos_ref, count_ref, core_ref, tiles_ref, source_ref, keep_ref, send_ref, acc_ref, held_ref, sems
):
    count = count_ref[0]
    core = core_ref[0]
    chunks = tiles_ref.shape[0] // UNROLL

    def fetch(k):
        slots = pl.ds(k * UNROLL, UNROLL)
        return pltpu.make_async_copy(tiles_ref.at[slots], held_ref.at[slots], sems.at[k])

    for k in range(chunks):
        fetch(k).start()
    acc_ref[...] = jnp.zeros_like(acc_ref)

    def chunk(k, carry):
        fetch(k).wait()

        @pl.when(k * UNROLL < count)
        def _():
            products = []
            for u in range(UNROLL):
                s = k * UNROLL + u
                j = pos_ref[1, s]
                picked = source_ref[pl.ds(2 * (j % (Y // 2)), 2), j // (Y // 2)].reshape(TILE, CH)
                picked = jnp.where(s < count, picked, jnp.zeros_like(picked))
                products.append(jnp.dot(held_ref[s], picked, preferred_element_type=jnp.float32))
            for u in range(UNROLL):
                i = pos_ref[0, k * UNROLL + u]
                acc_ref[i] += products[u].reshape(CORE, NODE, CH)

        return carry

    lax.fori_loop(0, chunks, chunk, 0)
    keep_ref[...] = acc_ref[:, core]
    send_ref[...] = acc_ref[:, 1 - core].astype(jnp.bfloat16)


def tile_product(positions, count, core, tiles, source):
    smem = pl.BlockSpec(memory_space=pltpu.SMEM)
    vmem = pl.BlockSpec(memory_space=pltpu.VMEM)
    return pl.pallas_call(
        tile_kernel,
        out_shape=(
            jax.ShapeDtypeStruct((ROW_TILES, NODE, CH), jnp.float32),
            jax.ShapeDtypeStruct((ROW_TILES, NODE, CH), jnp.bfloat16),
        ),
        in_specs=[smem, smem, smem, pl.BlockSpec(memory_space=pltpu.HBM), vmem],
        out_specs=(vmem, vmem),
        scratch_shapes=[
            pltpu.VMEM((ROW_TILES, CORE, NODE, CH), jnp.float32),
            pltpu.VMEM(tiles.shape, tiles.dtype),
            pltpu.SemaphoreType.DMA((tiles.shape[0] // UNROLL,)),
        ],
        compiler_params=pltpu.CompilerParams(vmem_limit_bytes=50 * 1024 * 1024),
        cost_estimate=pl.CostEstimate(
            flops=2 * 32 * TILE * TILE * CH, bytes_accessed=8 * 1024 * 1024, transcendentals=0
        ),
        name="tile_product",
    )(positions, count, core, tiles, source)


def pair_kernel(place_ref, keep_ref, arrived_ref, *refs):
    cot_refs, out_ref = refs[:X], refs[X]
    grad = jnp.zeros((CH, F), jnp.float32)
    for sx in range(X):
        for sz in range(Z_LO):
            k = (place_ref[0] + X - sx) % X * Z_LO + (place_ref[1] + Z_LO - sz) % Z_LO
            pair = (keep_ref[k] + arrived_ref[k].astype(jnp.float32)).astype(jnp.bfloat16)
            out_ref[k, :NODE] = pair
            grad += lax.dot_general(
                pair, cot_refs[sx][sz], (((0,), (0,)), ((), ())), preferred_element_type=jnp.float32
            )
    grad = grad.astype(jnp.bfloat16)
    per_side = CH // PIECE
    for k in range(ROW_TILES):
        if k < F // PIECE:
            side, part = divmod(k, per_side)
            out_ref[k, NODE:] = grad[part * PIECE : (part + 1) * PIECE, side * CH : (side + 1) * CH]
        else:
            out_ref[k, NODE:] = jnp.zeros((PIECE, CH), jnp.bfloat16)


def pair_stage(place, keep, arrived, cotangents):
    vmem = pl.BlockSpec(memory_space=pltpu.VMEM)
    return pl.pallas_call(
        pair_kernel,
        out_shape=jax.ShapeDtypeStruct((ROW_TILES, NODE + PIECE, CH), jnp.bfloat16),
        in_specs=[pl.BlockSpec(memory_space=pltpu.SMEM)] + [vmem] * (2 + X),
        out_specs=vmem,
        compiler_params=pltpu.CompilerParams(vmem_limit_bytes=16 * 1024 * 1024),
        cost_estimate=pl.CostEstimate(
            flops=2 * ROW_TILES * NODE * CH * F, bytes_accessed=3 * 1024 * 1024, transcendentals=0
        ),
        name="pair_stage",
    )(place, keep, arrived, *cotangents)


def node_kernel(parts_ref, degree_ref, weight_ref, out_ref, grad_ref):
    total = parts_ref[0].astype(jnp.float32)
    for k in range(1, ROW_TILES):
        total += parts_ref[k].astype(jnp.float32)
    grad_ref[...] = total[NODE:]
    aggregated = (
        total[:NODE] * lax.rsqrt(degree_ref[...].astype(jnp.float32))
    ).astype(jnp.bfloat16)
    out_ref[...] = jnp.dot(
        aggregated, weight_ref[...], preferred_element_type=jnp.float32
    ).astype(jnp.bfloat16)


def node_stage(parts, degree, weight):
    vmem = pl.BlockSpec(memory_space=pltpu.VMEM)
    return pl.pallas_call(
        node_kernel,
        out_shape=(
            jax.ShapeDtypeStruct((NODE, F), jnp.bfloat16),
            jax.ShapeDtypeStruct((PIECE, CH), jnp.float32),
        ),
        in_specs=[vmem] * 3,
        out_specs=(vmem, vmem),
        compiler_params=pltpu.CompilerParams(vmem_limit_bytes=8 * 1024 * 1024),
        cost_estimate=pl.CostEstimate(
            flops=2 * NODE * CH * F, bytes_accessed=1024 * 1024, transcendentals=NODE
        ),
        name="node_stage",
    )(parts, degree, weight)


def exchange(parts, axes):
    return lax.all_to_all(parts, axes, 0, 0)


def spread(piece, axes, n):
    return exchange(jnp.broadcast_to(piece[None], (n,) + piece.shape), axes)


def swap_cores(block):
    return lax.ppermute(block, "core", [(0, 1), (1, 0)])


def shifted(block, axis, n, shift):
    return lax.ppermute(block, axis, [(i, (i + shift) % n) for i in range(n)])


def per_device(features, out_degree, in_degree, tile_pos, tile_count, tiles, weight, cotangent):
    core = lax.axis_index("core")
    place = jnp.stack([lax.axis_index("x"), lax.axis_index("zl")])
    scaled = (
        features[0].astype(jnp.float32) * lax.rsqrt(out_degree[0].astype(jnp.float32))[:, None]
    ).astype(jnp.bfloat16)
    over_z = lax.all_gather(scaled, "zh", axis=0)
    copies = jnp.broadcast_to(over_z[None], (Y,) + over_z.shape)
    copies, cotangent, in_degree = lax.optimization_barrier((copies, cotangent, in_degree))
    source = exchange(copies, "y")

    scaled_cot = (
        cotangent[0].astype(jnp.float32)
        * lax.rsqrt(in_degree[0].astype(jnp.float32))[:, None]
    ).astype(jnp.bfloat16)
    over_zl = jnp.stack(
        [scaled_cot] + [shifted(scaled_cot, "zl", Z_LO, s) for s in range(1, Z_LO)]
    )
    cotangents = [over_zl] + [shifted(over_zl, "x", X, s) for s in range(1, X)]
    source, *cotangents = lax.optimization_barrier((source, *cotangents))

    keep, send = tile_product(
        tile_pos[0, 0].T, tile_count[0], core.reshape(1), tiles[0, 0], source
    )
    arrived = swap_cores(send)
    parts = exchange(pair_stage(place, keep, arrived, cotangents), ("x", "zl"))

    output, piece = node_stage(parts, in_degree[0][:, None], weight)

    piece = (piece + swap_cores(piece)).astype(jnp.bfloat16)
    piece = jnp.sum(spread(piece, ROW, N_ROW).astype(jnp.float32), axis=0).astype(jnp.bfloat16)
    pieces = spread(piece, ("x", "zl"), ROW_TILES)
    grad = pieces[: F // PIECE].reshape(F // CH, CH, CH).astype(jnp.float32)
    grad_weight = jnp.concatenate([grad[k] for k in range(F // CH)], axis=1)
    return (output[None], grad_weight)


def solution(mesh):
    fine = Mesh(mesh.devices.reshape(Z_HI, Y, X, Z_LO, CORE), ROW + COL)
    return jax.shard_map(
        per_device,
        mesh=fine,
        in_specs=(
            P(COL, ROW, None),
            P(COL, ROW),
            P(ROW, COL),
            P(ROW, COL, None, None),
            P(ROW, COL),
            P(ROW, COL, None, None, None),
            P(),
            P(ROW, COL, None),
        ),
        out_specs=(P(ROW, COL, None), P()),
        check_vma=False,
    )
```

time: 145 us -> 138 us (0.952)
  the two profiles are of different devices: /device:TPU:1 before, /device:TPU:8 now
where the time goes in v2:
time: 138 us; the launch traced here: 137 us
  blocking collectives  66.8 us (48%)
  starting transfers between devices  34.4 us (25%)
  waiting for transfers between devices  21.1 us (15%)
  Pallas kernels  6.25 us (5%)
  other arithmetic  4.84 us (4%)
  local copies, waits for them, and re-layouts  2.09 us (2%)
  between operations  1.45 us (1%)
    all_to_all x2, blocking collectives, exchange(): return lax.all_to_all(parts, axes, 0, 0)  42.3 us
    all_gather x1, blocking collectives, per_device(): over_z = lax.all_gather(scaled, 'zh', axis=0)  24.5 us
    ppermute x5, starting transfers between devices, shifted(): return lax.ppermute(block, axis, [(i, (i + shift) % n) for i in range(n)])  18.1 us
    all_to_all x2, starting transfers between devices, exchange(): return lax.all_to_all(parts, axes, 0, 0)  12.5 us
    all_to_all x2, waiting for transfers between devices, exchange(): return lax.all_to_all(parts, axes, 0, 0)  12.4 us
    ppermute x5, waiting for transfers between devices, shifted(): return lax.ppermute(block, axis, [(i, (i + shift) % n) for i in range(n)])  5.93 us
    ppermute x2, starting transfers between devices, swap_cores(): return lax.ppermute(block, 'core', [(0, 1), (1, 0)])  3.83 us
    pallas_call x1, Pallas kernels, tile_product(): pl.pallas_call(tile_kernel, out_shape=(jax.ShapeDtypeStruct((ROW_TILES, N...  3.64 us
  transfers between devices with their start and end apart: 9, of which 6 were waited for; matrix products, arithmetic and copies ran while one was open for 2% of the time, Pallas kernels for 0%

profile of v2, /device:TPU:8, one launch (start us, length us, event | category | flops | bytes accessed | tf_op | source)
XLA Modules:
  0.0 136.9 jit_solution(7058094711399099676)
XLA Ops:
  1.3 0.8 multiply_convert_fusion
  2.1 24.5 %all_gather.4 = bf16[4,128,128]{2,1,0:T(8,128)(2,1)S(1)} all-gather(bf16[1,128,128]{2,1,0:T(8,128)(2,1)S(1)} %multiply_convert_fusion), channel_id=1, replica_groups=mesh['zh'=4,'y'=8,'x'=4,'zl'=3,'core'=2] {'zh'}, dimensions={0}, use_global_device_ids=true | all-gather | bytes 163840 | tf_op jit(solution)/shard_map/all_gather | solution.py:172
  26.6 1.2 broadcast_in_dim.8
  27.9 7.5 %all-to-all-start = ((bf16[8,4,128,128]{3,2,1,0:T(8,128)(2,1)}), bf16[8,4,128,128]{3,2,1,0:T(8,128)(2,1)S(1)}, u32[]{:S(2)}, u32[]{:S(2)}) async-start(bf16[8,4,128,128]{3,2,1,0:T(8,128)(2,1)} %broadcast_in_dim.8), calls=%async_computation | async-start | bytes 2097152 | tf_op jit(solution)/shard_map/all_to_all | solution.py:151
  36.1 0.9 fusion.2
  37.0 3.9 %collective-permute-start = (bf16[128,256]{1,0:T(8,128)(2,1)S(1)}, bf16[128,256]{1,0:T(8,128)(2,1)S(1)}, u32[]{:S(2)}, u32[]{:S(2)}) collective-permute-start(bf16[128,256]{1,0:T(8,128)(2,1)S(1)} %fusion.2), channel_id=1, source_target_pairs={{0,2},{2,4},{4,0},{1,3},{3,5},{5,1},{6,8},{8,10},{10,6},{7,9},{9,1... | collective-permute-start | bytes 196616 | tf_op jit(solution)/shard_map/ppermute | solution.py:163
  40.9 2.8 %collective-permute-start.1 = (bf16[128,256]{1,0:T(8,128)(2,1)S(1)}, bf16[128,256]{1,0:T(8,128)(2,1)S(1)}, u32[]{:S(2)}, u32[]{:S(2)}) collective-permute-start(bf16[128,256]{1,0:T(8,128)(2,1)S(1)} %fusion.2), channel_id=1, source_target_pairs={{0,4},{2,0},{4,2},{1,5},{3,1},{5,3},{6,10},{8,6},{10,8},{7,11},{9,... | collective-permute-start | bytes 196616 | tf_op jit(solution)/shard_map/ppermute | solution.py:163
  43.8 0.9 fusion
  44.7 2.4 %collective-permute-done.1 = bf16[128,256]{1,0:T(8,128)(2,1)S(1)} collective-permute-done((bf16[128,256]{1,0:T(8,128)(2,1)S(1)}, bf16[128,256]{1,0:T(8,128)(2,1)S(1)}, u32[]{:S(2)}, u32[]{:S(2)}) %collective-permute-start.1) | collective-permute-done | bytes 65568 | tf_op jit(solution)/shard_map/ppermute | solution.py:163
  47.1 3.4 %collective-permute-start.2 = (bf16[3,128,256]{2,1,0:T(8,128)(2,1)S(1)}, bf16[3,128,256]{2,1,0:T(8,128)(2,1)S(1)}, u32[]{:S(2)}, u32[]{:S(2)}) collective-permute-start(bf16[3,128,256]{2,1,0:T(8,128)(2,1)S(1)} %pad_maximum_fusion.refs_0_), channel_id=1, source_target_pairs={{0,6},{6,12},{12,18},{18,0},{1,7},{7,13},{13,19},{19,1},{2,8},{8,1... | collective-permute-start | bytes 589832 | tf_op jit(solution)/shard_map/ppermute | solution.py:163
  50.5 4.6 %collective-permute-start.3 = (bf16[3,128,256]{2,1,0:T(8,128)(2,1)S(1)}, bf16[3,128,256]{2,1,0:T(8,128)(2,1)S(1)}, u32[]{:S(2)}, u32[]{:S(2)}) collective-permute-start(bf16[3,128,256]{2,1,0:T(8,128)(2,1)S(1)} %pad_maximum_fusion.refs_0_), channel_id=1, source_target_pairs={{0,12},{6,18},{12,0},{18,6},{1,13},{7,19},{13,1},{19,7},{2,14},{8,... | collective-permute-start | bytes 589832 | tf_op jit(solution)/shard_map/ppermute | solution.py:163
  55.2 3.3 %collective-permute-start.4 = (bf16[3,128,256]{2,1,0:T(8,128)(2,1)S(1)}, bf16[3,128,256]{2,1,0:T(8,128)(2,1)S(1)}, u32[]{:S(2)}, u32[]{:S(2)}) collective-permute-start(bf16[3,128,256]{2,1,0:T(8,128)(2,1)S(1)} %pad_maximum_fusion.refs_0_), channel_id=1, source_target_pairs={{0,18},{6,0},{12,6},{18,12},{1,19},{7,1},{13,7},{19,13},{2,20},{8,... | collective-permute-start | bytes 589832 | tf_op jit(solution)/shard_map/ppermute | solution.py:163
  59.6 3.1 %collective-permute-done.4.refs_3_ = bf16[3,128,256]{2,1,0:T(8,128)(2,1)S(1)} collective-permute-done((bf16[3,128,256]{2,1,0:T(8,128)(2,1)S(1)}, bf16[3,128,256]{2,1,0:T(8,128)(2,1)S(1)}, u32[]{:S(2)}, u32[]{:S(2)}) %collective-permute-start.4) | collective-permute-done | bytes 196640 | tf_op jit(solution)/shard_map/ppermute | solution.py:163
  63.4 3.6 %tile_product.1 = (f32[12,128,128]{2,1,0:T(8,128)S(1)}, bf16[12,128,128]{2,1,0:T(8,128)(2,1)S(1)}) custom-call(s32[2,32]{1,0:T(2,128)S(1)} %bitcast.25, s32[1]{0:T(128)} %bitcast.24.count_ref, s32[1]{0:T(128)} %bitcast.5.core_ref, bf16[32,256,256]{2,1,0:T(8,128)(2,1)} %bitcast.26, bf16[8,4,128,128]{3,2,1,0:T(8,128)(2,1)S(1)} %all-to-all-done.source_ref), custom_call_target="tpu_custom_call" | custom-call | flops 536870912 | bytes 8388608 | tf_op jit(solution)/shard_map/tile_product/pallas_call | solution.py:62
  67.1 1.9 %collective-permute-start.5 = (bf16[12,128,128]{2,1,0:T(8,128)(2,1)S(1)}, bf16[12,128,128]{2,1,0:T(8,128)(2,1)S(1)}, u32[]{:S(2)}, u32[]{:S(2)}) collective-permute-start(bf16[12,128,128]{2,1,0:T(8,128)(2,1)S(1)} %get-tuple-element.19), channel_id=1, source_target_pairs={{0,1},{1,0},{2,3},{3,2},{4,5},{5,4},{6,7},{7,6},{8,9},{9,8},{10,11... | collective-permute-start | bytes 1179656 | tf_op jit(solution)/shard_map/ppermute | solution.py:159
  69.1 1.6 %collective-permute-done.5.arrived_ref = bf16[12,128,128]{2,1,0:T(8,128)(2,1)S(1)} collective-permute-done((bf16[12,128,128]{2,1,0:T(8,128)(2,1)S(1)}, bf16[12,128,128]{2,1,0:T(8,128)(2,1)S(1)}, u32[]{:S(2)}, u32[]{:S(2)}) %collective-permute-start.5) | collective-permute-done | bytes 393248 | tf_op jit(solution)/shard_map/ppermute | solution.py:159
  70.7 1.8 %pair_stage.1 = bf16[12,160,128]{2,1,0:T(8,128)(2,1)} custom-call(s32[2]{0:T(128)S(1)} %pad_add_fusion.place_ref, f32[12,128,128]{2,1,0:T(8,128)S(1)} %get-tuple-element.18.keep_ref, bf16[12,128,128]{2,1,0:T(8,128)(2,1)S(1)} %collective-permute-done.5.arrived_ref, bf16[3,128,256]{2,1,0:T(8,128)(2,1)S(1)} %pad_maximum_fusion.refs_0_, ...), custom_call_target="tpu_custom_call" | custom-call | flops 100663296 | bytes 3145728 | tf_op jit(solution)/shard_map/pair_stage/pallas_call | solution.py:106
  72.4 4.9 %all-to-all-start.1 = ((bf16[12,160,128]{2,1,0:T(8,128)(2,1)}), bf16[12,160,128]{2,1,0:T(8,128)(2,1)S(1)}, u32[]{:S(2)}, u32[]{:S(2)}) async-start(bf16[12,160,128]{2,1,0:T(8,128)(2,1)} %pair_stage.1), calls=%async_computation.1 | async-start | bytes 983040 | tf_op jit(solution)/shard_map/all_to_all | solution.py:151
  77.5 12.4 %all-to-all-done.1.parts_ref = bf16[12,160,128]{2,1,0:T(8,128)(2,1)S(1)} async-done(((bf16[12,160,128]{2,1,0:T(8,128)(2,1)}), bf16[12,160,128]{2,1,0:T(8,128)(2,1)S(1)}, u32[]{:S(2)}, u32[]{:S(2)}) %all-to-all-start.1) | async-done | bytes 491552 | tf_op jit(solution)/shard_map/all_to_all | solution.py:151
  89.9 0.8 node_stage.1
  90.7 1.9 %collective-permute-start.6 = (f32[32,128]{1,0:T(8,128)S(1)}, f32[32,128]{1,0:T(8,128)S(1)}, u32[]{:S(2)}, u32[]{:S(2)}) collective-permute-start(f32[32,128]{1,0:T(8,128)S(1)} %get-tuple-element.25), channel_id=1, source_target_pairs={{0,1},{1,0},{2,3},{3,2},{4,5},{5,4},{6,7},{7,6},{8,9},{9,8},{10,11... | collective-permute-start | bytes 49160 | tf_op jit(solution)/shard_map/ppermute | solution.py:159
  92.6 1.1 collective-permute-done.6
  93.8 32.2 %all_to_all.20 = bf16[32,32,128]{2,1,0:T(8,128)(2,1)S(1)} all-to-all(bf16[32,32,128]{2,1,0:T(8,128)(2,1)S(1)} %broadcast_in_dim.10), channel_id=1, replica_groups=mesh['zh'=4,'y'=8,'x'=4,'zl'=3,'core'=2] {'zh','y'}, dimensions={0} | all-to-all | bytes 524288 | tf_op jit(solution)/shard_map/all_to_all | solution.py:151
  126.1 10.2 %all_to_all.21 = bf16[12,32,128]{2,1,0:T(8,128)(2,1)S(1)} all-to-all(bf16[12,32,128]{2,1,0:T(8,128)(2,1)S(1)} %broadcast_in_dim.11), channel_id=1, replica_groups=mesh['zh'=4,'y'=8,'x'=4,'zl'=3,'core'=2] {'x','zl'}, dimensions={0} | all-to-all | bytes 196608 | tf_op jit(solution)/shard_map/all_to_all | solution.py:151
  (22 shorter events, 3.4 us)
Async XLA Ops:
  27.9 34.9 %all-to-all-start = ((bf16[8,4,128,128]{3,2,1,0:T(8,128)(2,1)}), bf16[8,4,128,128]{3,2,1,0:T(8,128)(2,1)S(1)}, u32[]{:S(2)}, u32[]{:S(2)}) async-start(bf16[8,4,128,128]{3,2,1,0:T(8,128)(2,1)} %broadcast_in_dim.8), calls=%async_computation | async-start | bytes 2097152 | tf_op jit(solution)/shard_map/all_to_all | solution.py:151
  37.0 7.7 %collective-permute-start = (bf16[128,256]{1,0:T(8,128)(2,1)S(1)}, bf16[128,256]{1,0:T(8,128)(2,1)S(1)}, u32[]{:S(2)}, u32[]{:S(2)}) collective-permute-start(bf16[128,256]{1,0:T(8,128)(2,1)S(1)} %fusion.2), channel_id=1, source_target_pairs={{0,2},{2,4},{4,0},{1,3},{3,5},{5,1},{6,8},{8,10},{10,6},{7,9},{9,1... | collective-permute-start | bytes 196616 | tf_op jit(solution)/shard_map/ppermute | solution.py:163
  40.9 6.2 %collective-permute-start.1 = (bf16[128,256]{1,0:T(8,128)(2,1)S(1)}, bf16[128,256]{1,0:T(8,128)(2,1)S(1)}, u32[]{:S(2)}, u32[]{:S(2)}) collective-permute-start(bf16[128,256]{1,0:T(8,128)(2,1)S(1)} %fusion.2), channel_id=1, source_target_pairs={{0,4},{2,0},{4,2},{1,5},{3,1},{5,3},{6,10},{8,6},{10,8},{7,11},{9,... | collective-permute-start | bytes 196616 | tf_op jit(solution)/shard_map/ppermute | solution.py:163
  47.1 12.1 %collective-permute-start.2 = (bf16[3,128,256]{2,1,0:T(8,128)(2,1)S(1)}, bf16[3,128,256]{2,1,0:T(8,128)(2,1)S(1)}, u32[]{:S(2)}, u32[]{:S(2)}) collective-permute-start(bf16[3,128,256]{2,1,0:T(8,128)(2,1)S(1)} %pad_maximum_fusion.refs_0_), channel_id=1, source_target_pairs={{0,6},{6,12},{12,18},{18,0},{1,7},{7,13},{13,19},{19,1},{2,8},{8,1... | collective-permute-start | bytes 589832 | tf_op jit(solution)/shard_map/ppermute | solution.py:163
  50.5 9.1 %collective-permute-start.3 = (bf16[3,128,256]{2,1,0:T(8,128)(2,1)S(1)}, bf16[3,128,256]{2,1,0:T(8,128)(2,1)S(1)}, u32[]{:S(2)}, u32[]{:S(2)}) collective-permute-start(bf16[3,128,256]{2,1,0:T(8,128)(2,1)S(1)} %pad_maximum_fusion.refs_0_), channel_id=1, source_target_pairs={{0,12},{6,18},{12,0},{18,6},{1,13},{7,19},{13,1},{19,7},{2,14},{8,... | collective-permute-start | bytes 589832 | tf_op jit(solution)/shard_map/ppermute | solution.py:163
  55.2 7.6 %collective-permute-start.4 = (bf16[3,128,256]{2,1,0:T(8,128)(2,1)S(1)}, bf16[3,128,256]{2,1,0:T(8,128)(2,1)S(1)}, u32[]{:S(2)}, u32[]{:S(2)}) collective-permute-start(bf16[3,128,256]{2,1,0:T(8,128)(2,1)S(1)} %pad_maximum_fusion.refs_0_), channel_id=1, source_target_pairs={{0,18},{6,0},{12,6},{18,12},{1,19},{7,1},{13,7},{19,13},{2,20},{8,... | collective-permute-start | bytes 589832 | tf_op jit(solution)/shard_map/ppermute | solution.py:163
  62.7 0.7 copy-start.1
  63.4 14.0 %copy-start.2 = (s32[1,128]{1,0:T(1,128)S(1)}, s32[1,128]{1,0:T(1,128)}, u32[]{:S(2)}) copy-start(s32[1,128]{1,0:T(1,128)} %param.10) | copy-start | bytes 1540
  63.4 26.5 %copy-start = (bf16[128,256]{1,0:T(8,128)(2,1)S(1)}, bf16[128,256]{1,0:T(8,128)(2,1)}, u32[]{:S(2)}) copy-start(bf16[128,256]{1,0:T(8,128)(2,1)} %weight_ref.1) | copy-start | bytes 196612
  67.1 3.6 %collective-permute-start.5 = (bf16[12,128,128]{2,1,0:T(8,128)(2,1)S(1)}, bf16[12,128,128]{2,1,0:T(8,128)(2,1)S(1)}, u32[]{:S(2)}, u32[]{:S(2)}) collective-permute-start(bf16[12,128,128]{2,1,0:T(8,128)(2,1)S(1)} %get-tuple-element.19), channel_id=1, source_target_pairs={{0,1},{1,0},{2,3},{3,2},{4,5},{5,4},{6,7},{7,6},{8,9},{9,8},{10,11... | collective-permute-start | bytes 1179656 | tf_op jit(solution)/shard_map/ppermute | solution.py:159
  72.4 17.4 %all-to-all-start.1 = ((bf16[12,160,128]{2,1,0:T(8,128)(2,1)}), bf16[12,160,128]{2,1,0:T(8,128)(2,1)S(1)}, u32[]{:S(2)}, u32[]{:S(2)}) async-start(bf16[12,160,128]{2,1,0:T(8,128)(2,1)} %pair_stage.1), calls=%async_computation.1 | async-start | bytes 983040 | tf_op jit(solution)/shard_map/all_to_all | solution.py:151
  90.7 3.1 %collective-permute-start.6 = (f32[32,128]{1,0:T(8,128)S(1)}, f32[32,128]{1,0:T(8,128)S(1)}, u32[]{:S(2)}, u32[]{:S(2)}) collective-permute-start(f32[32,128]{1,0:T(8,128)S(1)} %get-tuple-element.25), channel_id=1, source_target_pairs={{0,1},{1,0},{2,3},{3,2},{4,5},{5,4},{6,7},{7,6},{8,9},{9,8},{10,11... | collective-permute-start | bytes 49160 | tf_op jit(solution)/shard_map/ppermute | solution.py:159

commit v3 on v2

--- a/solution.py
+++ b/solution.py
@@ -13,6 +13,7 @@
 CH = 128
 F = 256
 ROW_TILES = X * Z_LO
+COL_TILES = Z_HI * Y * NODE // TILE
 N_ROW = Z_HI * Y
 PIECE = 32
 UNROLL = 4
@@ -41,12 +42,12 @@
             products = []
             for u in range(UNROLL):
                 s = k * UNROLL + u
-                j = pos_ref[1, s]
+                j = pos_ref[s] % COL_TILES
                 picked = source_ref[pl.ds(2 * (j % (Y // 2)), 2), j // (Y // 2)].reshape(TILE, CH)
                 picked = jnp.where(s < count, picked, jnp.zeros_like(picked))
                 products.append(jnp.dot(held_ref[s], picked, preferred_element_type=jnp.float32))
             for u in range(UNROLL):
-                i = pos_ref[0, k * UNROLL + u]
+                i = pos_ref[k * UNROLL + u] // COL_TILES
                 acc_ref[i] += products[u].reshape(CORE, NODE, CH)
 
         return carry
@@ -171,31 +172,36 @@
     ).astype(jnp.bfloat16)
     over_z = lax.all_gather(scaled, "zh", axis=0)
     copies = jnp.broadcast_to(over_z[None], (Y,) + over_z.shape)
-    copies, cotangent, in_degree = lax.optimization_barrier((copies, cotangent, in_degree))
+    copies, cotangent, in_degree, tile_pos = lax.optimization_barrier(
+        (copies, cotangent, in_degree, tile_pos)
+    )
     source = exchange(copies, "y")
 
     scaled_cot = (
-        cotangent[0].astype(jnp.float32)
-        * lax.rsqrt(in_degree[0].astype(jnp.float32))[:, None]
-    ).astype(jnp.bfloat16)
-    over_zl = jnp.stack(
+        cotangent.astype(jnp.float32) * lax.rsqrt(in_degree.astype(jnp.float32))[:, :, None]
+    ).astype(jnp.bfloat16)
+    over_zl = jnp.concatenate(
         [scaled_cot] + [shifted(scaled_cot, "zl", Z_LO, s) for s in range(1, Z_LO)]
     )
     cotangents = [over_zl] + [shifted(over_zl, "x", X, s) for s in range(1, X)]
-    source, *cotangents = lax.optimization_barrier((source, *cotangents))
+    places = tile_pos[0, 0, :, 0] * COL_TILES + tile_pos[0, 0, :, 1]
+    source, places, *cotangents = lax.optimization_barrier((source, places, *cotangents))
 
     keep, send = tile_product(
-        tile_pos[0, 0].T, tile_count[0], core.reshape(1), tiles[0, 0], source
+        places, tile_count[0], core.reshape(1), tiles[0, 0], source
     )
     arrived = swap_cores(send)
     parts = exchange(pair_stage(place, keep, arrived, cotangents), ("x", "zl"))
 
     output, piece = node_stage(parts, in_degree[0][:, None], weight)
 
-    piece = (piece + swap_cores(piece)).astype(jnp.bfloat16)
+    halves = piece.reshape(CORE, PIECE // CORE, CH)
+    own = lax.dynamic_index_in_dim(halves, core, 0, keepdims=False)
+    other = lax.dynamic_index_in_dim(halves, 1 - core, 0, keepdims=False)
+    piece = (own + swap_cores(other)).astype(jnp.bfloat16)
     piece = jnp.sum(spread(piece, ROW, N_ROW).astype(jnp.float32), axis=0).astype(jnp.bfloat16)
-    pieces = spread(piece, ("x", "zl"), ROW_TILES)
-    grad = pieces[: F // PIECE].reshape(F // CH, CH, CH).astype(jnp.float32)
+    pieces = spread(piece, COL, CORE * ROW_TILES)
+    grad = pieces[: CORE * F // PIECE].reshape(F // CH, CH, CH).astype(jnp.float32)
     grad_weight = jnp.concatenate([grad[k] for k in range(F // CH)], axis=1)
     return (output[None], grad_weight)
 

time: 138 us -> 135 us (0.978)
  the two profiles are of different devices: /device:TPU:8 before, /device:TPU:1 now
where the time goes in v3:
time: 135 us; the launch traced here: 134 us
  blocking collectives  62.1 us (46%)
  starting transfers between devices  38.5 us (29%)
  waiting for transfers between devices  19.8 us (15%)
  Pallas kernels  6.28 us (5%)
  other arithmetic  4.66 us (3%)
  between operations  1.44 us (1%)
  local copies, waits for them, and re-layouts  1.38 us (1%)
    all_to_all x2, blocking collectives, exchange(): return lax.all_to_all(parts, axes, 0, 0)  39 us
    all_gather x1, blocking collectives, per_device(): over_z = lax.all_gather(scaled, 'zh', axis=0)  23.1 us
    ppermute x5, starting transfers between devices, shifted(): return lax.ppermute(block, axis, [(i, (i + shift) % n) for i in range(n)])  16.7 us
    all_to_all x2, starting transfers between devices, exchange(): return lax.all_to_all(parts, axes, 0, 0)  12.9 us
    all_to_all x2, waiting for transfers between devices, exchange(): return lax.all_to_all(parts, axes, 0, 0)  12.7 us
    ppermute x2, starting transfers between devices, swap_cores(): return lax.ppermute(block, 'core', [(0, 1), (1, 0)])  8.88 us
    ppermute x5, waiting for transfers between devices, shifted(): return lax.ppermute(block, axis, [(i, (i + shift) % n) for i in range(n)])  5.06 us
    pallas_call x1, Pallas kernels, tile_product(): pl.pallas_call(tile_kernel, out_shape=(jax.ShapeDtypeStruct((ROW_TILES, N...  3.68 us
  transfers between devices with their start and end apart: 9, of which 7 were waited for; matrix products, arithmetic and copies ran while one was open for 2% of the time, Pallas kernels for 0%

profile of v3, /device:TPU:1, one launch (start us, length us, event | category | flops | bytes accessed | tf_op | source)
XLA Modules:
  0.0 134.2 jit_solution(2890785720989109091)
XLA Ops:
  1.3 0.8 multiply_convert_fusion.1
  2.1 23.1 %all_gather.4 = bf16[4,128,128]{2,1,0:T(8,128)(2,1)S(1)} all-gather(bf16[1,128,128]{2,1,0:T(8,128)(2,1)S(1)} %multiply_convert_fusion.1), channel_id=1, replica_groups=mesh['zh'=4,'y'=8,'x'=4,'zl'=3,'core'=2] {'zh'}, dimensions={0}, use_global_device_ids=true | all-gather | bytes 163840 | tf_op jit(solution)/shard_map/all_gather | solution.py:173
  25.3 1.2 broadcast_in_dim.8
  26.5 6.8 %all-to-all-start = ((bf16[8,4,128,128]{3,2,1,0:T(8,128)(2,1)}), bf16[8,4,128,128]{3,2,1,0:T(8,128)(2,1)S(1)}, u32[]{:S(2)}, u32[]{:S(2)}) async-start(bf16[8,4,128,128]{3,2,1,0:T(8,128)(2,1)} %broadcast_in_dim.8), calls=%async_computation | async-start | bytes 2097152 | tf_op jit(solution)/shard_map/all_to_all | solution.py:152
  34.0 0.9 multiply_convert_fusion
  34.9 3.3 %collective-permute-start = (bf16[1,128,256]{2,1,0:T(8,128)(2,1)S(1)}, bf16[1,128,256]{2,1,0:T(8,128)(2,1)S(1)}, u32[]{:S(2)}, u32[]{:S(2)}) collective-permute-start(bf16[1,128,256]{2,1,0:T(8,128)(2,1)S(1)} %multiply_convert_fusion), channel_id=1, source_target_pairs={{0,2},{2,4},{4,0},{1,3},{3,5},{5,1},{6,8},{8,10},{10,6},{7,9},{9,1... | collective-permute-start | bytes 196616 | tf_op jit(solution)/shard_map/ppermute | solution.py:164
  38.2 2.9 %collective-permute-start.1 = (bf16[1,128,256]{2,1,0:T(8,128)(2,1)S(1)}, bf16[1,128,256]{2,1,0:T(8,128)(2,1)S(1)}, u32[]{:S(2)}, u32[]{:S(2)}) collective-permute-start(bf16[1,128,256]{2,1,0:T(8,128)(2,1)S(1)} %multiply_convert_fusion), channel_id=1, source_target_pairs={{0,4},{2,0},{4,2},{1,5},{3,1},{5,3},{6,10},{8,6},{10,8},{7,11},{9,... | collective-permute-start | bytes 196616 | tf_op jit(solution)/shard_map/ppermute | solution.py:164
  41.8 1.7 %collective-permute-done.1 = bf16[1,128,256]{2,1,0:T(8,128)(2,1)S(1)} collective-permute-done((bf16[1,128,256]{2,1,0:T(8,128)(2,1)S(1)}, bf16[1,128,256]{2,1,0:T(8,128)(2,1)S(1)}, u32[]{:S(2)}, u32[]{:S(2)}) %collective-permute-start.1) | collective-permute-done | bytes 65568 | tf_op jit(solution)/shard_map/ppermute | solution.py:164
  43.5 3.1 %collective-permute-start.2 = (bf16[3,128,256]{2,1,0:T(8,128)(2,1)S(1)}, bf16[3,128,256]{2,1,0:T(8,128)(2,1)S(1)}, u32[]{:S(2)}, u32[]{:S(2)}) collective-permute-start(bf16[3,128,256]{2,1,0:T(8,128)(2,1)S(1)} %pad_maximum_fusion.refs_0_), channel_id=1, source_target_pairs={{0,6},{6,12},{12,18},{18,0},{1,7},{7,13},{13,19},{19,1},{2,8},{8,1... | collective-permute-start | bytes 589832 | tf_op jit(solution)/shard_map/ppermute | solution.py:164
  46.6 4.4 %collective-permute-start.3 = (bf16[3,128,256]{2,1,0:T(8,128)(2,1)S(1)}, bf16[3,128,256]{2,1,0:T(8,128)(2,1)S(1)}, u32[]{:S(2)}, u32[]{:S(2)}) collective-permute-start(bf16[3,128,256]{2,1,0:T(8,128)(2,1)S(1)} %pad_maximum_fusion.refs_0_), channel_id=1, source_target_pairs={{0,12},{6,18},{12,0},{18,6},{1,13},{7,19},{13,1},{19,7},{2,14},{8,... | collective-permute-start | bytes 589832 | tf_op jit(solution)/shard_map/ppermute | solution.py:164
  51.0 3.1 %collective-permute-start.4 = (bf16[3,128,256]{2,1,0:T(8,128)(2,1)S(1)}, bf16[3,128,256]{2,1,0:T(8,128)(2,1)S(1)}, u32[]{:S(2)}, u32[]{:S(2)}) collective-permute-start(bf16[3,128,256]{2,1,0:T(8,128)(2,1)S(1)} %pad_maximum_fusion.refs_0_), channel_id=1, source_target_pairs={{0,18},{6,0},{12,6},{18,12},{1,19},{7,1},{13,7},{19,13},{2,20},{8,... | collective-permute-start | bytes 589832 | tf_op jit(solution)/shard_map/ppermute | solution.py:164
  55.0 3.2 %collective-permute-done.4.refs_3_ = bf16[3,128,256]{2,1,0:T(8,128)(2,1)S(1)} collective-permute-done((bf16[3,128,256]{2,1,0:T(8,128)(2,1)S(1)}, bf16[3,128,256]{2,1,0:T(8,128)(2,1)S(1)}, u32[]{:S(2)}, u32[]{:S(2)}) %collective-permute-start.4) | collective-permute-done | bytes 196640 | tf_op jit(solution)/shard_map/ppermute | solution.py:164
  58.2 1.9 %all-to-all-done.source_ref = bf16[8,4,128,128]{3,2,1,0:T(8,128)(2,1)S(1)} async-done(((bf16[8,4,128,128]{3,2,1,0:T(8,128)(2,1)}), bf16[8,4,128,128]{3,2,1,0:T(8,128)(2,1)S(1)}, u32[]{:S(2)}, u32[]{:S(2)}) %all-to-all-start) | async-done | bytes 1048608 | tf_op jit(solution)/shard_map/all_to_all | solution.py:152
  60.1 3.7 %tile_product.1 = (f32[12,128,128]{2,1,0:T(8,128)S(1)}, bf16[12,128,128]{2,1,0:T(8,128)(2,1)S(1)}) custom-call(s32[32]{0:T(128)S(1)} %add_bitcast_fusion.pos_ref, s32[1]{0:T(128)} %bitcast.22.count_ref, s32[1]{0:T(128)} %bitcast.6.core_ref, bf16[32,256,256]{2,1,0:T(8,128)(2,1)} %bitcast.25, bf16[8,4,128,128]{3,2,1,0:T(8,128)(2,1)S(1)} %all-to-all-done.source_ref), custom_call_target="tpu_custom_call" | custom-call | flops 536870912 | bytes 8388608 | tf_op jit(solution)/shard_map/tile_product/pallas_call | solution.py:63
  63.8 4.7 %collective-permute-start.5 = (bf16[12,128,128]{2,1,0:T(8,128)(2,1)S(1)}, bf16[12,128,128]{2,1,0:T(8,128)(2,1)S(1)}, u32[]{:S(2)}, u32[]{:S(2)}) collective-permute-start(bf16[12,128,128]{2,1,0:T(8,128)(2,1)S(1)} %get-tuple-element.23), channel_id=1, source_target_pairs={{0,1},{1,0},{2,3},{3,2},{4,5},{5,4},{6,7},{7,6},{8,9},{9,8},{10,11... | collective-permute-start | bytes 1179656 | tf_op jit(solution)/shard_map/ppermute | solution.py:160
  68.6 1.2 collective-permute-done.5.arrived_ref
  69.9 1.8 %pair_stage.1 = bf16[12,160,128]{2,1,0:T(8,128)(2,1)} custom-call(s32[2]{0:T(128)S(1)} %pad_add_fusion.place_ref, f32[12,128,128]{2,1,0:T(8,128)S(1)} %get-tuple-element.22.keep_ref, bf16[12,128,128]{2,1,0:T(8,128)(2,1)S(1)} %collective-permute-done.5.arrived_ref, bf16[3,128,256]{2,1,0:T(8,128)(2,1)S(1)} %pad_maximum_fusion.refs_0_, ...), custom_call_target="tpu_custom_call" | custom-call | flops 100663296 | bytes 3145728 | tf_op jit(solution)/shard_map/pair_stage/pallas_call | solution.py:107
  71.6 6.1 %all-to-all-start.1 = ((bf16[12,160,128]{2,1,0:T(8,128)(2,1)}), bf16[12,160,128]{2,1,0:T(8,128)(2,1)S(1)}, u32[]{:S(2)}, u32[]{:S(2)}) async-start(bf16[12,160,128]{2,1,0:T(8,128)(2,1)} %pair_stage.1), calls=%async_computation.1 | async-start | bytes 983040 | tf_op jit(solution)/shard_map/all_to_all | solution.py:152
  77.8 10.8 %all-to-all-done.1.parts_ref = bf16[12,160,128]{2,1,0:T(8,128)(2,1)S(1)} async-done(((bf16[12,160,128]{2,1,0:T(8,128)(2,1)}), bf16[12,160,128]{2,1,0:T(8,128)(2,1)S(1)}, u32[]{:S(2)}, u32[]{:S(2)}) %all-to-all-start.1) | async-done | bytes 491552 | tf_op jit(solution)/shard_map/all_to_all | solution.py:152
  88.6 0.8 node_stage.1
  89.5 4.1 %collective-permute-start.6 = (f32[16,128]{1,0:T(8,128)S(1)}, f32[16,128]{1,0:T(8,128)S(1)}, u32[]{:S(2)}, u32[]{:S(2)}) collective-permute-start(f32[16,128]{1,0:T(8,128)S(1)} %dynamic-slice_bitcast_fusion), channel_id=1, source_target_pairs={{0,1},{1,0},{2,3},{3,2},{4,5},{5,4},{6,7},{7,6},{8,9},{9,8},{10,11... | collective-permute-start | bytes 24584 | tf_op jit(solution)/shard_map/ppermute | solution.py:160
  93.6 0.8 collective-permute-done.6
  94.5 27.3 %all_to_all.20 = bf16[32,16,128]{2,1,0:T(8,128)(2,1)S(1)} all-to-all(bf16[32,16,128]{2,1,0:T(8,128)(2,1)S(1)} %broadcast_in_dim.10), channel_id=1, replica_groups=mesh['zh'=4,'y'=8,'x'=4,'zl'=3,'core'=2] {'zh','y'}, dimensions={0} | all-to-all | bytes 262144 | tf_op jit(solution)/shard_map/all_to_all | solution.py:152
  121.8 11.7 %all_to_all.21 = bf16[24,16,128]{2,1,0:T(8,128)(2,1)S(1)} all-to-all(bf16[24,16,128]{2,1,0:T(8,128)(2,1)S(1)} %broadcast_in_dim.11), channel_id=1, replica_groups=mesh['zh'=4,'y'=8,'x'=4,'zl'=3,'core'=2] {'x','zl','core'}, dimensions={0} | all-to-all | bytes 196608 | tf_op jit(solution)/shard_map/all_to_all | solution.py:152
  (21 shorter events, 3.2 us)
Async XLA Ops:
  26.5 33.6 %all-to-all-start = ((bf16[8,4,128,128]{3,2,1,0:T(8,128)(2,1)}), bf16[8,4,128,128]{3,2,1,0:T(8,128)(2,1)S(1)}, u32[]{:S(2)}, u32[]{:S(2)}) async-start(bf16[8,4,128,128]{3,2,1,0:T(8,128)(2,1)} %broadcast_in_dim.8), calls=%async_computation | async-start | bytes 2097152 | tf_op jit(solution)/shard_map/all_to_all | solution.py:152
  34.9 6.9 %collective-permute-start = (bf16[1,128,256]{2,1,0:T(8,128)(2,1)S(1)}, bf16[1,128,256]{2,1,0:T(8,128)(2,1)S(1)}, u32[]{:S(2)}, u32[]{:S(2)}) collective-permute-start(bf16[1,128,256]{2,1,0:T(8,128)(2,1)S(1)} %multiply_convert_fusion), channel_id=1, source_target_pairs={{0,2},{2,4},{4,0},{1,3},{3,5},{5,1},{6,8},{8,10},{10,6},{7,9},{9,1... | collective-permute-start | bytes 196616 | tf_op jit(solution)/shard_map/ppermute | solution.py:164
  38.2 5.3 %collective-permute-start.1 = (bf16[1,128,256]{2,1,0:T(8,128)(2,1)S(1)}, bf16[1,128,256]{2,1,0:T(8,128)(2,1)S(1)}, u32[]{:S(2)}, u32[]{:S(2)}) collective-permute-start(bf16[1,128,256]{2,1,0:T(8,128)(2,1)S(1)} %multiply_convert_fusion), channel_id=1, source_target_pairs={{0,4},{2,0},{4,2},{1,5},{3,1},{5,3},{6,10},{8,6},{10,8},{7,11},{9,... | collective-permute-start | bytes 196616 | tf_op jit(solution)/shard_map/ppermute | solution.py:164
  43.5 11.3 %collective-permute-start.2 = (bf16[3,128,256]{2,1,0:T(8,128)(2,1)S(1)}, bf16[3,128,256]{2,1,0:T(8,128)(2,1)S(1)}, u32[]{:S(2)}, u32[]{:S(2)}) collective-permute-start(bf16[3,128,256]{2,1,0:T(8,128)(2,1)S(1)} %pad_maximum_fusion.refs_0_), channel_id=1, source_target_pairs={{0,6},{6,12},{12,18},{18,0},{1,7},{7,13},{13,19},{19,1},{2,8},{8,1... | collective-permute-start | bytes 589832 | tf_op jit(solution)/shard_map/ppermute | solution.py:164
  46.6 8.4 %collective-permute-start.3 = (bf16[3,128,256]{2,1,0:T(8,128)(2,1)S(1)}, bf16[3,128,256]{2,1,0:T(8,128)(2,1)S(1)}, u32[]{:S(2)}, u32[]{:S(2)}) collective-permute-start(bf16[3,128,256]{2,1,0:T(8,128)(2,1)S(1)} %pad_maximum_fusion.refs_0_), channel_id=1, source_target_pairs={{0,12},{6,18},{12,0},{18,6},{1,13},{7,19},{13,1},{19,7},{2,14},{8,... | collective-permute-start | bytes 589832 | tf_op jit(solution)/shard_map/ppermute | solution.py:164
  51.0 7.2 %collective-permute-start.4 = (bf16[3,128,256]{2,1,0:T(8,128)(2,1)S(1)}, bf16[3,128,256]{2,1,0:T(8,128)(2,1)S(1)}, u32[]{:S(2)}, u32[]{:S(2)}) collective-permute-start(bf16[3,128,256]{2,1,0:T(8,128)(2,1)S(1)} %pad_maximum_fusion.refs_0_), channel_id=1, source_target_pairs={{0,18},{6,0},{12,6},{18,12},{1,19},{7,1},{13,7},{19,13},{2,20},{8,... | collective-permute-start | bytes 589832 | tf_op jit(solution)/shard_map/ppermute | solution.py:164
  60.1 17.6 %copy-start.1 = (s32[1,128]{1,0:T(1,128)S(1)}, s32[1,128]{1,0:T(1,128)}, u32[]{:S(2)}) copy-start(s32[1,128]{1,0:T(1,128)} %param.10) | copy-start | bytes 1540
  60.1 28.5 %copy-start = (bf16[128,256]{1,0:T(8,128)(2,1)S(1)}, bf16[128,256]{1,0:T(8,128)(2,1)}, u32[]{:S(2)}) copy-start(bf16[128,256]{1,0:T(8,128)(2,1)} %weight_ref.1) | copy-start | bytes 196612
  63.8 6.1 %collective-permute-start.5 = (bf16[12,128,128]{2,1,0:T(8,128)(2,1)S(1)}, bf16[12,128,128]{2,1,0:T(8,128)(2,1)S(1)}, u32[]{:S(2)}, u32[]{:S(2)}) collective-permute-start(bf16[12,128,128]{2,1,0:T(8,128)(2,1)S(1)} %get-tuple-element.23), channel_id=1, source_target_pairs={{0,1},{1,0},{2,3},{3,2},{4,5},{5,4},{6,7},{7,6},{8,9},{9,8},{10,11... | collective-permute-start | bytes 1179656 | tf_op jit(solution)/shard_map/ppermute | solution.py:160
  71.6 17.0 %all-to-all-start.1 = ((bf16[12,160,128]{2,1,0:T(8,128)(2,1)}), bf16[12,160,128]{2,1,0:T(8,128)(2,1)S(1)}, u32[]{:S(2)}, u32[]{:S(2)}) async-start(bf16[12,160,128]{2,1,0:T(8,128)(2,1)} %pair_stage.1), calls=%async_computation.1 | async-start | bytes 983040 | tf_op jit(solution)/shard_map/all_to_all | solution.py:152
  89.5 4.9 %collective-permute-start.6 = (f32[16,128]{1,0:T(8,128)S(1)}, f32[16,128]{1,0:T(8,128)S(1)}, u32[]{:S(2)}, u32[]{:S(2)}) collective-permute-start(f32[16,128]{1,0:T(8,128)S(1)} %dynamic-slice_bitcast_fusion), channel_id=1, source_target_pairs={{0,1},{1,0},{2,3},{3,2},{4,5},{5,4},{6,7},{7,6},{8,9},{9,8},{10,11... | collective-permute-start | bytes 24584 | tf_op jit(solution)/shard_map/ppermute | solution.py:160

commit v4 on v3

--- a/solution.py
+++ b/solution.py
@@ -16,7 +16,30 @@
 COL_TILES = Z_HI * Y * NODE // TILE
 N_ROW = Z_HI * Y
 PIECE = 32
-UNROLL = 4
+UNROLL = 8
+
+
+def scale_kernel(features_ref, degree_ref, copies_ref):
+    factor = lax.rsqrt(degree_ref[...].astype(jnp.float32))
+    factor = jnp.broadcast_to(factor, (NODE, NODE)).T
+    scaled = (features_ref[...].astype(jnp.float32) * factor).astype(jnp.bfloat16)
+    for k in range(Z_HI):
+        copies_ref[k] = scaled
+
+
+def scaled_copies(features, degree):
+    vmem = pl.BlockSpec(memory_space=pltpu.VMEM)
+    return pl.pallas_call(
+        scale_kernel,
+        out_shape=jax.ShapeDtypeStruct((Z_HI, NODE, CH), jnp.bfloat16),
+        in_specs=[vmem, vmem],
+        out_specs=vmem,
+        compiler_params=pltpu.CompilerParams(vmem_limit_bytes=8 * 1024 * 1024),
+        cost_estimate=pl.CostEstimate(
+            flops=NODE * CH, bytes_accessed=256 * 1024, transcendentals=NODE
+        ),
+        name="scaled_copies",
+    )(features, degree)
 
 
 def tile_kernel(
@@ -39,16 +62,13 @@
 
         @pl.when(k * UNROLL < count)
         def _():
-            products = []
             for u in range(UNROLL):
                 s = k * UNROLL + u
-                j = pos_ref[s] % COL_TILES
+                i, j = pos_ref[s] // COL_TILES, pos_ref[s] % COL_TILES
                 picked = source_ref[pl.ds(2 * (j % (Y // 2)), 2), j // (Y // 2)].reshape(TILE, CH)
                 picked = jnp.where(s < count, picked, jnp.zeros_like(picked))
-                products.append(jnp.dot(held_ref[s], picked, preferred_element_type=jnp.float32))
-            for u in range(UNROLL):
-                i = pos_ref[k * UNROLL + u] // COL_TILES
-                acc_ref[i] += products[u].reshape(CORE, NODE, CH)
+                product = jnp.dot(held_ref[s], picked, preferred_element_type=jnp.float32)
+                acc_ref[i] += product.reshape(CORE, NODE, CH)
 
         return carry
 
@@ -88,7 +108,7 @@
         for sz in range(Z_LO):
             k = (place_ref[0] + X - sx) % X * Z_LO + (place_ref[1] + Z_LO - sz) % Z_LO
             pair = (keep_ref[k] + arrived_ref[k].astype(jnp.float32)).astype(jnp.bfloat16)
-            out_ref[k, :NODE] = pair
+            out_ref[k % Z_LO * X + k // Z_LO, :NODE] = pair
             grad += lax.dot_general(
                 pair, cot_refs[sx][sz], (((0,), (0,)), ((), ())), preferred_element_type=jnp.float32
             )
@@ -167,10 +187,7 @@
 def per_device(features, out_degree, in_degree, tile_pos, tile_count, tiles, weight, cotangent):
     core = lax.axis_index("core")
     place = jnp.stack([lax.axis_index("x"), lax.axis_index("zl")])
-    scaled = (
-        features[0].astype(jnp.float32) * lax.rsqrt(out_degree[0].astype(jnp.float32))[:, None]
-    ).astype(jnp.bfloat16)
-    over_z = lax.all_gather(scaled, "zh", axis=0)
+    over_z = exchange(scaled_copies(features[0], out_degree), "zh")
     copies = jnp.broadcast_to(over_z[None], (Y,) + over_z.shape)
     copies, cotangent, in_degree, tile_pos = lax.optimization_barrier(
         (copies, cotangent, in_degree, tile_pos)
@@ -191,7 +208,7 @@
         places, tile_count[0], core.reshape(1), tiles[0, 0], source
     )
     arrived = swap_cores(send)
-    parts = exchange(pair_stage(place, keep, arrived, cotangents), ("x", "zl"))
+    parts = exchange(pair_stage(place, keep, arrived, cotangents), ("zl", "x"))
 
     output, piece = node_stage(parts, in_degree[0][:, None], weight)
 
@@ -200,7 +217,7 @@
     other = lax.dynamic_index_in_dim(halves, 1 - core, 0, keepdims=False)
     piece = (own + swap_cores(other)).astype(jnp.bfloat16)
     piece = jnp.sum(spread(piece, ROW, N_ROW).astype(jnp.float32), axis=0).astype(jnp.bfloat16)
-    pieces = spread(piece, COL, CORE * ROW_TILES)
+    pieces = spread(piece, ("zl", "x", "core"), CORE * ROW_TILES)
     grad = pieces[: CORE * F // PIECE].reshape(F // CH, CH, CH).astype(jnp.float32)
     grad_weight = jnp.concatenate([grad[k] for k in range(F // CH)], axis=1)
     return (output[None], grad_weight)

time: 135 us -> 134 us (level)
  starting transfers between devices: 38.5 us -> 41.7 us
  waiting for transfers between devices: 19.8 us -> 16.8 us
  other arithmetic: 4.66 us -> 2.41 us
  local copies, waits for them, and re-layouts: 1.38 us -> 2.8 us
    all_to_all x2 -> x3, blocking collectives: 39 us -> 62.5 us  [exchange(): return lax.all_to_all(parts, axes, 0, 0)]
    all_gather x1 -> x0, blocking collectives: 23.1 us -> none  [per_device(): over_z = lax.all_gather(scaled, 'zh', axis=0)]
    ppermute x2, starting transfers between devices: 8.88 us -> 11.9 us  [swap_cores(): return lax.ppermute(block, 'core', [(0, 1), (1, 0)])]
    all_to_all x2, waiting for transfers between devices: 12.7 us -> 9.77 us  [exchange(): return lax.all_to_all(parts, axes, 0, 0)]
    unnamed x4 -> x10, local copies, waits for them, and re-layouts: 0.01 us -> 1.42 us
  transfers between devices with their start and end apart: 9 -> 9, of which waited for: 7 -> 7; matrix products, arithmetic and copies ran while one was open for 2% -> 1% of each run, Pallas kernels for 0% -> 0%
where the time goes in v4:
time: 134 us; the launch traced here: 133 us
  blocking collectives  62.5 us (47%)
  starting transfers between devices  41.7 us (31%)
  waiting for transfers between devices  16.8 us (13%)
  Pallas kernels  5.55 us (4%)
  local copies, waits for them, and re-layouts  2.8 us (2%)
  other arithmetic  2.41 us (2%)
  between operations  1.48 us (1%)
    all_to_all x3, blocking collectives, exchange(): return lax.all_to_all(parts, axes, 0, 0)  62.5 us
    ppermute x5, starting transfers between devices, shifted(): return lax.ppermute(block, axis, [(i, (i + shift) % n) for i in range(n)])  17 us
    all_to_all x2, starting transfers between devices, exchange(): return lax.all_to_all(parts, axes, 0, 0)  12.8 us
    ppermute x2, starting transfers between devices, swap_cores(): return lax.ppermute(block, 'core', [(0, 1), (1, 0)])  11.9 us
    all_to_all x2, waiting for transfers between devices, exchange(): return lax.all_to_all(parts, axes, 0, 0)  9.77 us
    ppermute x5, waiting for transfers between devices, shifted(): return lax.ppermute(block, axis, [(i, (i + shift) % n) for i in range(n)])  5.01 us
    pallas_call x1, Pallas kernels, tile_product(): pl.pallas_call(tile_kernel, out_shape=(jax.ShapeDtypeStruct((ROW_TILES, N...  2.84 us
  transfers between devices with their start and end apart: 9, of which 7 were waited for; matrix products, arithmetic and copies ran while one was open for 1% of the time, Pallas kernels for 0%

profile of v4, /device:TPU:1, one launch (start us, length us, event | category | flops | bytes accessed | tf_op | source)
XLA Modules:
  0.0 133.3 jit_solution(3976981377789948928)
XLA Ops:
  0.6 0.8 copy-done.1
  2.2 24.6 %all_to_all.25 = bf16[4,128,128]{2,1,0:T(8,128)(2,1)S(1)} all-to-all(bf16[4,128,128]{2,1,0:T(8,128)(2,1)S(1)} %scaled_copies.1), channel_id=1, replica_groups=mesh['zh'=4,'y'=8,'x'=4,'zl'=3,'core'=2] {'zh'}, dimensions={0} | all-to-all | bytes 262144 | tf_op jit(solution)/shard_map/all_to_all | solution.py:172
  26.8 1.2 broadcast_in_dim.8
  28.0 6.8 %all-to-all-start.1 = ((bf16[8,4,128,128]{3,2,1,0:T(8,128)(2,1)}), bf16[8,4,128,128]{3,2,1,0:T(8,128)(2,1)S(1)}, u32[]{:S(2)}, u32[]{:S(2)}) async-start(bf16[8,4,128,128]{3,2,1,0:T(8,128)(2,1)} %broadcast_in_dim.8), calls=%async_computation.1 | async-start | bytes 2097152 | tf_op jit(solution)/shard_map/all_to_all | solution.py:172
  35.5 0.9 multiply_convert_fusion
  36.4 3.1 %collective-permute-start = (bf16[1,128,256]{2,1,0:T(8,128)(2,1)S(1)}, bf16[1,128,256]{2,1,0:T(8,128)(2,1)S(1)}, u32[]{:S(2)}, u32[]{:S(2)}) collective-permute-start(bf16[1,128,256]{2,1,0:T(8,128)(2,1)S(1)} %multiply_convert_fusion), channel_id=1, source_target_pairs={{0,2},{2,4},{4,0},{1,3},{3,5},{5,1},{6,8},{8,10},{10,6},{7,9},{9,1... | collective-permute-start | bytes 196616 | tf_op jit(solution)/shard_map/ppermute | solution.py:184
  39.5 3.4 %collective-permute-start.1 = (bf16[1,128,256]{2,1,0:T(8,128)(2,1)S(1)}, bf16[1,128,256]{2,1,0:T(8,128)(2,1)S(1)}, u32[]{:S(2)}, u32[]{:S(2)}) collective-permute-start(bf16[1,128,256]{2,1,0:T(8,128)(2,1)S(1)} %multiply_convert_fusion), channel_id=1, source_target_pairs={{0,4},{2,0},{4,2},{1,5},{3,1},{5,3},{6,10},{8,6},{10,8},{7,11},{9,... | collective-permute-start | bytes 196616 | tf_op jit(solution)/shard_map/ppermute | solution.py:184
  43.5 1.5 %collective-permute-done.1 = bf16[1,128,256]{2,1,0:T(8,128)(2,1)S(1)} collective-permute-done((bf16[1,128,256]{2,1,0:T(8,128)(2,1)S(1)}, bf16[1,128,256]{2,1,0:T(8,128)(2,1)S(1)}, u32[]{:S(2)}, u32[]{:S(2)}) %collective-permute-start.1) | collective-permute-done | bytes 65568 | tf_op jit(solution)/shard_map/ppermute | solution.py:184
  45.1 3.1 %collective-permute-start.2 = (bf16[3,128,256]{2,1,0:T(8,128)(2,1)S(1)}, bf16[3,128,256]{2,1,0:T(8,128)(2,1)S(1)}, u32[]{:S(2)}, u32[]{:S(2)}) collective-permute-start(bf16[3,128,256]{2,1,0:T(8,128)(2,1)S(1)} %pad_maximum_fusion.refs_0_), channel_id=1, source_target_pairs={{0,6},{6,12},{12,18},{18,0},{1,7},{7,13},{13,19},{19,1},{2,8},{8,1... | collective-permute-start | bytes 589832 | tf_op jit(solution)/shard_map/ppermute | solution.py:184
  48.2 4.4 %collective-permute-start.3 = (bf16[3,128,256]{2,1,0:T(8,128)(2,1)S(1)}, bf16[3,128,256]{2,1,0:T(8,128)(2,1)S(1)}, u32[]{:S(2)}, u32[]{:S(2)}) collective-permute-start(bf16[3,128,256]{2,1,0:T(8,128)(2,1)S(1)} %pad_maximum_fusion.refs_0_), channel_id=1, source_target_pairs={{0,12},{6,18},{12,0},{18,6},{1,13},{7,19},{13,1},{19,7},{2,14},{8,... | collective-permute-start | bytes 589832 | tf_op jit(solution)/shard_map/ppermute | solution.py:184
  52.6 3.1 %collective-permute-start.4 = (bf16[3,128,256]{2,1,0:T(8,128)(2,1)S(1)}, bf16[3,128,256]{2,1,0:T(8,128)(2,1)S(1)}, u32[]{:S(2)}, u32[]{:S(2)}) collective-permute-start(bf16[3,128,256]{2,1,0:T(8,128)(2,1)S(1)} %pad_maximum_fusion.refs_0_), channel_id=1, source_target_pairs={{0,18},{6,0},{12,6},{18,12},{1,19},{7,1},{13,7},{19,13},{2,20},{8,... | collective-permute-start | bytes 589832 | tf_op jit(solution)/shard_map/ppermute | solution.py:184
  56.3 2.9 %collective-permute-done.4.refs_3_ = bf16[3,128,256]{2,1,0:T(8,128)(2,1)S(1)} collective-permute-done((bf16[3,128,256]{2,1,0:T(8,128)(2,1)S(1)}, bf16[3,128,256]{2,1,0:T(8,128)(2,1)S(1)}, u32[]{:S(2)}, u32[]{:S(2)}) %collective-permute-start.4) | collective-permute-done | bytes 196640 | tf_op jit(solution)/shard_map/ppermute | solution.py:184
  59.2 1.3 %all-to-all-done.1.source_ref = bf16[8,4,128,128]{3,2,1,0:T(8,128)(2,1)S(1)} async-done(((bf16[8,4,128,128]{3,2,1,0:T(8,128)(2,1)}), bf16[8,4,128,128]{3,2,1,0:T(8,128)(2,1)S(1)}, u32[]{:S(2)}, u32[]{:S(2)}) %all-to-all-start.1) | async-done | bytes 1048608 | tf_op jit(solution)/shard_map/all_to_all | solution.py:172
  60.5 2.8 %tile_product.1 = (f32[12,128,128]{2,1,0:T(8,128)S(1)}, bf16[12,128,128]{2,1,0:T(8,128)(2,1)S(1)}) custom-call(s32[32]{0:T(128)S(1)} %add_bitcast_fusion.pos_ref, s32[1]{0:T(128)} %bitcast.21.count_ref, s32[1]{0:T(128)} %bitcast.6.core_ref, bf16[32,256,256]{2,1,0:T(8,128)(2,1)} %bitcast.25, bf16[8,4,128,128]{3,2,1,0:T(8,128)(2,1)S(1)} %all-to-all-done.1.source_ref), custom_call_target="tpu_custom_call" | custom-call | flops 536870912 | bytes 8388608 | tf_op jit(solution)/shard_map/tile_product/pallas_call | solution.py:83
  63.4 7.1 %collective-permute-start.5 = (bf16[12,128,128]{2,1,0:T(8,128)(2,1)S(1)}, bf16[12,128,128]{2,1,0:T(8,128)(2,1)S(1)}, u32[]{:S(2)}, u32[]{:S(2)}) collective-permute-start(bf16[12,128,128]{2,1,0:T(8,128)(2,1)S(1)} %get-tuple-element.23), channel_id=1, source_target_pairs={{0,1},{1,0},{2,3},{3,2},{4,5},{5,4},{6,7},{7,6},{8,9},{9,8},{10,11... | collective-permute-start | bytes 1179656 | tf_op jit(solution)/shard_map/ppermute | solution.py:180
  70.5 1.2 collective-permute-done.5.arrived_ref
  71.8 1.8 %pair_stage.1 = bf16[12,160,128]{2,1,0:T(8,128)(2,1)} custom-call(s32[2]{0:T(128)S(1)} %pad_add_fusion.place_ref, f32[12,128,128]{2,1,0:T(8,128)S(1)} %get-tuple-element.22.keep_ref, bf16[12,128,128]{2,1,0:T(8,128)(2,1)S(1)} %collective-permute-done.5.arrived_ref, bf16[3,128,256]{2,1,0:T(8,128)(2,1)S(1)} %pad_maximum_fusion.refs_0_, ...), custom_call_target="tpu_custom_call" | custom-call | flops 100663296 | bytes 3145728 | tf_op jit(solution)/shard_map/pair_stage/pallas_call | solution.py:127
  73.5 6.0 %all-to-all-start.2 = ((bf16[12,160,128]{2,1,0:T(8,128)(2,1)}), bf16[12,160,128]{2,1,0:T(8,128)(2,1)S(1)}, u32[]{:S(2)}, u32[]{:S(2)}) async-start(bf16[12,160,128]{2,1,0:T(8,128)(2,1)} %pair_stage.1), calls=%async_computation.2 | async-start | bytes 983040 | tf_op jit(solution)/shard_map/all_to_all | solution.py:172
  79.6 8.4 %all-to-all-done.2.parts_ref = bf16[12,160,128]{2,1,0:T(8,128)(2,1)S(1)} async-done(((bf16[12,160,128]{2,1,0:T(8,128)(2,1)}), bf16[12,160,128]{2,1,0:T(8,128)(2,1)S(1)}, u32[]{:S(2)}, u32[]{:S(2)}) %all-to-all-start.2) | async-done | bytes 491552 | tf_op jit(solution)/shard_map/all_to_all | solution.py:172
  88.1 0.8 node_stage.1
  88.9 4.8 %collective-permute-start.6 = (f32[16,128]{1,0:T(8,128)S(1)}, f32[16,128]{1,0:T(8,128)S(1)}, u32[]{:S(2)}, u32[]{:S(2)}) collective-permute-start(f32[16,128]{1,0:T(8,128)S(1)} %dynamic-slice_bitcast_fusion), channel_id=1, source_target_pairs={{0,1},{1,0},{2,3},{3,2},{4,5},{5,4},{6,7},{7,6},{8,9},{9,8},{10,11... | collective-permute-start | bytes 24584 | tf_op jit(solution)/shard_map/ppermute | solution.py:180
  93.8 0.8 collective-permute-done.6
  94.6 24.3 %all_to_all.26 = bf16[32,16,128]{2,1,0:T(8,128)(2,1)S(1)} all-to-all(bf16[32,16,128]{2,1,0:T(8,128)(2,1)S(1)} %broadcast_in_dim.10), channel_id=1, replica_groups=mesh['zh'=4,'y'=8,'x'=4,'zl'=3,'core'=2] {'zh','y'}, dimensions={0} | all-to-all | bytes 262144 | tf_op jit(solution)/shard_map/all_to_all | solution.py:172
  118.9 13.6 %all_to_all.27 = bf16[24,16,128]{2,1,0:T(8,128)(2,1)S(1)} all-to-all(bf16[24,16,128]{2,1,0:T(8,128)(2,1)S(1)} %broadcast_in_dim.11), channel_id=1, replica_groups=mesh['zh'=4,'y'=8,'x'=4,'zl'=3,'core'=2] {'zl','x','core'}, dimensions={0} | all-to-all | bytes 196608 | tf_op jit(solution)/shard_map/all_to_all | solution.py:172
  (26 shorter events, 3.0 us)
Async XLA Ops:
  0.6 55.0 %copy-start.4 = (s32[1,1,32,2]{2,3,1,0:T(2,128)S(1)}, s32[1,1,32,2]{2,3,1,0:T(2,128)}, u32[]{:S(2)}) copy-start(s32[1,1,32,2]{2,3,1,0:T(2,128)} %param.11) | copy-start | bytes 772
  0.6 0.8 copy-start.1
  1.4 0.7 copy-start.2
  28.0 32.5 %all-to-all-start.1 = ((bf16[8,4,128,128]{3,2,1,0:T(8,128)(2,1)}), bf16[8,4,128,128]{3,2,1,0:T(8,128)(2,1)S(1)}, u32[]{:S(2)}, u32[]{:S(2)}) async-start(bf16[8,4,128,128]{3,2,1,0:T(8,128)(2,1)} %broadcast_in_dim.8), calls=%async_computation.1 | async-start | bytes 2097152 | tf_op jit(solution)/shard_map/all_to_all | solution.py:172
  36.4 7.1 %collective-permute-start = (bf16[1,128,256]{2,1,0:T(8,128)(2,1)S(1)}, bf16[1,128,256]{2,1,0:T(8,128)(2,1)S(1)}, u32[]{:S(2)}, u32[]{:S(2)}) collective-permute-start(bf16[1,128,256]{2,1,0:T(8,128)(2,1)S(1)} %multiply_convert_fusion), channel_id=1, source_target_pairs={{0,2},{2,4},{4,0},{1,3},{3,5},{5,1},{6,8},{8,10},{10,6},{7,9},{9,1... | collective-permute-start | bytes 196616 | tf_op jit(solution)/shard_map/ppermute | solution.py:184
  39.5 5.6 %collective-permute-start.1 = (bf16[1,128,256]{2,1,0:T(8,128)(2,1)S(1)}, bf16[1,128,256]{2,1,0:T(8,128)(2,1)S(1)}, u32[]{:S(2)}, u32[]{:S(2)}) collective-permute-start(bf16[1,128,256]{2,1,0:T(8,128)(2,1)S(1)} %multiply_convert_fusion), channel_id=1, source_target_pairs={{0,4},{2,0},{4,2},{1,5},{3,1},{5,3},{6,10},{8,6},{10,8},{7,11},{9,... | collective-permute-start | bytes 196616 | tf_op jit(solution)/shard_map/ppermute | solution.py:184
  45.1 10.6 %collective-permute-start.2 = (bf16[3,128,256]{2,1,0:T(8,128)(2,1)S(1)}, bf16[3,128,256]{2,1,0:T(8,128)(2,1)S(1)}, u32[]{:S(2)}, u32[]{:S(2)}) collective-permute-start(bf16[3,128,256]{2,1,0:T(8,128)(2,1)S(1)} %pad_maximum_fusion.refs_0_), channel_id=1, source_target_pairs={{0,6},{6,12},{12,18},{18,0},{1,7},{7,13},{13,19},{19,1},{2,8},{8,1... | collective-permute-start | bytes 589832 | tf_op jit(solution)/shard_map/ppermute | solution.py:184
  48.2 8.1 %collective-permute-start.3 = (bf16[3,128,256]{2,1,0:T(8,128)(2,1)S(1)}, bf16[3,128,256]{2,1,0:T(8,128)(2,1)S(1)}, u32[]{:S(2)}, u32[]{:S(2)}) collective-permute-start(bf16[3,128,256]{2,1,0:T(8,128)(2,1)S(1)} %pad_maximum_fusion.refs_0_), channel_id=1, source_target_pairs={{0,12},{6,18},{12,0},{18,6},{1,13},{7,19},{13,1},{19,7},{2,14},{8,... | collective-permute-start | bytes 589832 | tf_op jit(solution)/shard_map/ppermute | solution.py:184
  52.6 6.6 %collective-permute-start.4 = (bf16[3,128,256]{2,1,0:T(8,128)(2,1)S(1)}, bf16[3,128,256]{2,1,0:T(8,128)(2,1)S(1)}, u32[]{:S(2)}, u32[]{:S(2)}) collective-permute-start(bf16[3,128,256]{2,1,0:T(8,128)(2,1)S(1)} %pad_maximum_fusion.refs_0_), channel_id=1, source_target_pairs={{0,18},{6,0},{12,6},{18,12},{1,19},{7,1},{13,7},{19,13},{2,20},{8,... | collective-permute-start | bytes 589832 | tf_op jit(solution)/shard_map/ppermute | solution.py:184
  60.5 19.0 %copy-start.3 = (s32[1,128]{1,0:T(1,128)S(1)}, s32[1,128]{1,0:T(1,128)}, u32[]{:S(2)}) copy-start(s32[1,128]{1,0:T(1,128)} %param.10) | copy-start | bytes 1540
  60.5 27.6 %copy-start = (bf16[128,256]{1,0:T(8,128)(2,1)S(1)}, bf16[128,256]{1,0:T(8,128)(2,1)}, u32[]{:S(2)}) copy-start(bf16[128,256]{1,0:T(8,128)(2,1)} %weight_ref.1) | copy-start | bytes 196612
  63.4 8.4 %collective-permute-start.5 = (bf16[12,128,128]{2,1,0:T(8,128)(2,1)S(1)}, bf16[12,128,128]{2,1,0:T(8,128)(2,1)S(1)}, u32[]{:S(2)}, u32[]{:S(2)}) collective-permute-start(bf16[12,128,128]{2,1,0:T(8,128)(2,1)S(1)} %get-tuple-element.23), channel_id=1, source_target_pairs={{0,1},{1,0},{2,3},{3,2},{4,5},{5,4},{6,7},{7,6},{8,9},{9,8},{10,11... | collective-permute-start | bytes 1179656 | tf_op jit(solution)/shard_map/ppermute | solution.py:180
  73.5 14.5 %all-to-all-start.2 = ((bf16[12,160,128]{2,1,0:T(8,128)(2,1)}), bf16[12,160,128]{2,1,0:T(8,128)(2,1)S(1)}, u32[]{:S(2)}, u32[]{:S(2)}) async-start(bf16[12,160,128]{2,1,0:T(8,128)(2,1)} %pair_stage.1), calls=%async_computation.2 | async-start | bytes 983040 | tf_op jit(solution)/shard_map/all_to_all | solution.py:172
  88.9 5.7 %collective-permute-start.6 = (f32[16,128]{1,0:T(8,128)S(1)}, f32[16,128]{1,0:T(8,128)S(1)}, u32[]{:S(2)}, u32[]{:S(2)}) collective-permute-start(f32[16,128]{1,0:T(8,128)S(1)} %dynamic-slice_bitcast_fusion), channel_id=1, source_target_pairs={{0,1},{1,0},{2,3},{3,2},{4,5},{5,4},{6,7},{7,6},{8,9},{9,8},{10,11... | collective-permute-start | bytes 24584 | tf_op jit(solution)/shard_map/ppermute | solution.py:180

commit v5 on v4

--- a/solution.py
+++ b/solution.py
@@ -212,11 +212,12 @@
 
     output, piece = node_stage(parts, in_degree[0][:, None], weight)
 
-    halves = piece.reshape(CORE, PIECE // CORE, CH)
-    own = lax.dynamic_index_in_dim(halves, core, 0, keepdims=False)
-    other = lax.dynamic_index_in_dim(halves, 1 - core, 0, keepdims=False)
-    piece = (own + swap_cores(other)).astype(jnp.bfloat16)
-    piece = jnp.sum(spread(piece, ROW, N_ROW).astype(jnp.float32), axis=0).astype(jnp.bfloat16)
+    halves = jnp.broadcast_to(
+        piece.astype(jnp.bfloat16).reshape(1, CORE, PIECE // CORE, CH),
+        (Y, CORE, PIECE // CORE, CH),
+    ).reshape(Y * CORE, PIECE // CORE, CH)
+    piece = jnp.sum(exchange(halves, ("y", "core")).astype(jnp.float32), axis=0)
+    piece = lax.psum(piece, "zh").astype(jnp.bfloat16)
     pieces = spread(piece, ("zl", "x", "core"), CORE * ROW_TILES)
     grad = pieces[: CORE * F // PIECE].reshape(F // CH, CH, CH).astype(jnp.float32)
     grad_weight = jnp.concatenate([grad[k] for k in range(F // CH)], axis=1)

time: 134 us -> 133 us (level)
  blocking collectives: 62.5 us -> 68.3 us
  starting transfers between devices: 41.7 us -> 36.3 us
    psum x0 -> x1, blocking collectives: none -> 12.2 us  [per_device(): piece = lax.psum(piece, 'zh').astype(jnp.bfloat16)]
    all_to_all x3, blocking collectives: 62.5 us -> 56.1 us  [exchange(): return lax.all_to_all(parts, axes, 0, 0)]
    ppermute x2 -> x1, starting transfers between devices: 11.9 us -> 7.47 us  [swap_cores(): return lax.ppermute(block, 'core', [(0, 1), (1, 0)])]
  transfers between devices with their start and end apart: 9 -> 8, of which waited for: 7 -> 6; matrix products, arithmetic and copies ran while one was open for 1% -> 1% of each run, Pallas kernels for 0% -> 0%
where the time goes in v5:
time: 133 us
  blocking collectives  68.3 us (51%)
  starting transfers between devices  36.3 us (27%)
  waiting for transfers between devices  15.7 us (12%)
  Pallas kernels  5.56 us (4%)
  local copies, waits for them, and re-layouts  2.79 us (2%)
  other arithmetic  2.39 us (2%)
  between operations  1.47 us (1%)
    all_to_all x3, blocking collectives, exchange(): return lax.all_to_all(parts, axes, 0, 0)  56.1 us
    ppermute x5, starting transfers between devices, shifted(): return lax.ppermute(block, axis, [(i, (i + shift) % n) for i in range(n)])  17 us
    psum x1, blocking collectives, per_device(): piece = lax.psum(piece, 'zh').astype(jnp.bfloat16)  12.2 us
    all_to_all x2, starting transfers between devices, exchange(): return lax.all_to_all(parts, axes, 0, 0)  11.8 us
    all_to_all x2, waiting for transfers between devices, exchange(): return lax.all_to_all(parts, axes, 0, 0)  9.48 us
    ppermute x1, starting transfers between devices, swap_cores(): return lax.ppermute(block, 'core', [(0, 1), (1, 0)])  7.47 us
    ppermute x5, waiting for transfers between devices, shifted(): return lax.ppermute(block, axis, [(i, (i + shift) % n) for i in range(n)])  5.01 us
    pallas_call x1, Pallas kernels, tile_product(): pl.pallas_call(tile_kernel, out_shape=(jax.ShapeDtypeStruct((ROW_TILES, N...  2.84 us
  transfers between devices with their start and end apart: 8, of which 6 were waited for; matrix products, arithmetic and copies ran while one was open for 1% of the time, Pallas kernels for 0%

profile of v5, /device:TPU:1, one launch (start us, length us, event | category | flops | bytes accessed | tf_op | source)
XLA Modules:
  0.0 132.5 jit_solution(9135030602984695259)
XLA Ops:
  0.6 0.8 copy-done.1
  2.2 24.6 %all_to_all.25 = bf16[4,128,128]{2,1,0:T(8,128)(2,1)S(1)} all-to-all(bf16[4,128,128]{2,1,0:T(8,128)(2,1)S(1)} %scaled_copies.1), channel_id=1, replica_groups=mesh['zh'=4,'y'=8,'x'=4,'zl'=3,'core'=2] {'zh'}, dimensions={0} | all-to-all | bytes 262144 | tf_op jit(solution)/shard_map/all_to_all | solution.py:172
  26.8 1.2 broadcast_in_dim.10
  28.0 6.8 %all-to-all-start.1 = ((bf16[8,4,128,128]{3,2,1,0:T(8,128)(2,1)}), bf16[8,4,128,128]{3,2,1,0:T(8,128)(2,1)S(1)}, u32[]{:S(2)}, u32[]{:S(2)}) async-start(bf16[8,4,128,128]{3,2,1,0:T(8,128)(2,1)} %broadcast_in_dim.10), calls=%async_computation.1 | async-start | bytes 2097152 | tf_op jit(solution)/shard_map/all_to_all | solution.py:172
  35.5 0.9 multiply_convert_fusion
  36.4 3.1 %collective-permute-start = (bf16[1,128,256]{2,1,0:T(8,128)(2,1)S(1)}, bf16[1,128,256]{2,1,0:T(8,128)(2,1)S(1)}, u32[]{:S(2)}, u32[]{:S(2)}) collective-permute-start(bf16[1,128,256]{2,1,0:T(8,128)(2,1)S(1)} %multiply_convert_fusion), channel_id=1, source_target_pairs={{0,2},{2,4},{4,0},{1,3},{3,5},{5,1},{6,8},{8,10},{10,6},{7,9},{9,1... | collective-permute-start | bytes 196616 | tf_op jit(solution)/shard_map/ppermute | solution.py:184
  39.5 3.4 %collective-permute-start.1 = (bf16[1,128,256]{2,1,0:T(8,128)(2,1)S(1)}, bf16[1,128,256]{2,1,0:T(8,128)(2,1)S(1)}, u32[]{:S(2)}, u32[]{:S(2)}) collective-permute-start(bf16[1,128,256]{2,1,0:T(8,128)(2,1)S(1)} %multiply_convert_fusion), channel_id=1, source_target_pairs={{0,4},{2,0},{4,2},{1,5},{3,1},{5,3},{6,10},{8,6},{10,8},{7,11},{9,... | collective-permute-start | bytes 196616 | tf_op jit(solution)/shard_map/ppermute | solution.py:184
  43.5 1.5 %collective-permute-done.1 = bf16[1,128,256]{2,1,0:T(8,128)(2,1)S(1)} collective-permute-done((bf16[1,128,256]{2,1,0:T(8,128)(2,1)S(1)}, bf16[1,128,256]{2,1,0:T(8,128)(2,1)S(1)}, u32[]{:S(2)}, u32[]{:S(2)}) %collective-permute-start.1) | collective-permute-done | bytes 65568 | tf_op jit(solution)/shard_map/ppermute | solution.py:184
  45.1 3.1 %collective-permute-start.2 = (bf16[3,128,256]{2,1,0:T(8,128)(2,1)S(1)}, bf16[3,128,256]{2,1,0:T(8,128)(2,1)S(1)}, u32[]{:S(2)}, u32[]{:S(2)}) collective-permute-start(bf16[3,128,256]{2,1,0:T(8,128)(2,1)S(1)} %pad_maximum_fusion.refs_0_), channel_id=1, source_target_pairs={{0,6},{6,12},{12,18},{18,0},{1,7},{7,13},{13,19},{19,1},{2,8},{8,1... | collective-permute-start | bytes 589832 | tf_op jit(solution)/shard_map/ppermute | solution.py:184
  48.2 4.4 %collective-permute-start.3 = (bf16[3,128,256]{2,1,0:T(8,128)(2,1)S(1)}, bf16[3,128,256]{2,1,0:T(8,128)(2,1)S(1)}, u32[]{:S(2)}, u32[]{:S(2)}) collective-permute-start(bf16[3,128,256]{2,1,0:T(8,128)(2,1)S(1)} %pad_maximum_fusion.refs_0_), channel_id=1, source_target_pairs={{0,12},{6,18},{12,0},{18,6},{1,13},{7,19},{13,1},{19,7},{2,14},{8,... | collective-permute-start | bytes 589832 | tf_op jit(solution)/shard_map/ppermute | solution.py:184
  52.6 3.1 %collective-permute-start.4 = (bf16[3,128,256]{2,1,0:T(8,128)(2,1)S(1)}, bf16[3,128,256]{2,1,0:T(8,128)(2,1)S(1)}, u32[]{:S(2)}, u32[]{:S(2)}) collective-permute-start(bf16[3,128,256]{2,1,0:T(8,128)(2,1)S(1)} %pad_maximum_fusion.refs_0_), channel_id=1, source_target_pairs={{0,18},{6,0},{12,6},{18,12},{1,19},{7,1},{13,7},{19,13},{2,20},{8,... | collective-permute-start | bytes 589832 | tf_op jit(solution)/shard_map/ppermute | solution.py:184
  56.3 2.9 %collective-permute-done.4.refs_3_ = bf16[3,128,256]{2,1,0:T(8,128)(2,1)S(1)} collective-permute-done((bf16[3,128,256]{2,1,0:T(8,128)(2,1)S(1)}, bf16[3,128,256]{2,1,0:T(8,128)(2,1)S(1)}, u32[]{:S(2)}, u32[]{:S(2)}) %collective-permute-start.4) | collective-permute-done | bytes 196640 | tf_op jit(solution)/shard_map/ppermute | solution.py:184
  59.2 1.3 %all-to-all-done.1.source_ref = bf16[8,4,128,128]{3,2,1,0:T(8,128)(2,1)S(1)} async-done(((bf16[8,4,128,128]{3,2,1,0:T(8,128)(2,1)}), bf16[8,4,128,128]{3,2,1,0:T(8,128)(2,1)S(1)}, u32[]{:S(2)}, u32[]{:S(2)}) %all-to-all-start.1) | async-done | bytes 1048608 | tf_op jit(solution)/shard_map/all_to_all | solution.py:172
  60.5 2.8 %tile_product.1 = (f32[12,128,128]{2,1,0:T(8,128)S(1)}, bf16[12,128,128]{2,1,0:T(8,128)(2,1)S(1)}) custom-call(s32[32]{0:T(128)S(1)} %add_bitcast_fusion.pos_ref, s32[1]{0:T(128)} %bitcast.16.count_ref, s32[1]{0:T(128)} %bitcast.6.core_ref, bf16[32,256,256]{2,1,0:T(8,128)(2,1)} %bitcast.18, bf16[8,4,128,128]{3,2,1,0:T(8,128)(2,1)S(1)} %all-to-all-done.1.source_ref), custom_call_target="tpu_custom_call" | custom-call | flops 536870912 | bytes 8388608 | tf_op jit(solution)/shard_map/tile_product/pallas_call | solution.py:83
  63.4 7.5 %collective-permute-start.5 = (bf16[12,128,128]{2,1,0:T(8,128)(2,1)S(1)}, bf16[12,128,128]{2,1,0:T(8,128)(2,1)S(1)}, u32[]{:S(2)}, u32[]{:S(2)}) collective-permute-start(bf16[12,128,128]{2,1,0:T(8,128)(2,1)S(1)} %get-tuple-element.23), channel_id=1, source_target_pairs={{0,1},{1,0},{2,3},{3,2},{4,5},{5,4},{6,7},{7,6},{8,9},{9,8},{10,11... | collective-permute-start | bytes 1179656 | tf_op jit(solution)/shard_map/ppermute | solution.py:180
  70.9 1.2 collective-permute-done.5.arrived_ref
  72.2 1.8 %pair_stage.1 = bf16[12,160,128]{2,1,0:T(8,128)(2,1)} custom-call(s32[2]{0:T(128)S(1)} %pad_add_fusion.place_ref, f32[12,128,128]{2,1,0:T(8,128)S(1)} %get-tuple-element.22.keep_ref, bf16[12,128,128]{2,1,0:T(8,128)(2,1)S(1)} %collective-permute-done.5.arrived_ref, bf16[3,128,256]{2,1,0:T(8,128)(2,1)S(1)} %pad_maximum_fusion.refs_0_, ...), custom_call_target="tpu_custom_call" | custom-call | flops 100663296 | bytes 3145728 | tf_op jit(solution)/shard_map/pair_stage/pallas_call | solution.py:127
  73.9 5.0 %all-to-all-start.2 = ((bf16[12,160,128]{2,1,0:T(8,128)(2,1)}), bf16[12,160,128]{2,1,0:T(8,128)(2,1)S(1)}, u32[]{:S(2)}, u32[]{:S(2)}) async-start(bf16[12,160,128]{2,1,0:T(8,128)(2,1)} %pair_stage.1), calls=%async_computation.2 | async-start | bytes 983040 | tf_op jit(solution)/shard_map/all_to_all | solution.py:172
  79.0 8.1 %all-to-all-done.2.parts_ref = bf16[12,160,128]{2,1,0:T(8,128)(2,1)S(1)} async-done(((bf16[12,160,128]{2,1,0:T(8,128)(2,1)}), bf16[12,160,128]{2,1,0:T(8,128)(2,1)S(1)}, u32[]{:S(2)}, u32[]{:S(2)}) %all-to-all-start.2) | async-done | bytes 491552 | tf_op jit(solution)/shard_map/all_to_all | solution.py:172
  87.2 0.8 node_stage.1
  88.1 17.8 %all_to_all.26 = bf16[16,16,128]{2,1,0:T(8,128)(2,1)S(1)} all-to-all(bf16[16,16,128]{2,1,0:T(8,128)(2,1)S(1)} %bitcast.19), channel_id=1, replica_groups=mesh['zh'=4,'y'=8,'x'=4,'zl'=3,'core'=2] {'y','core'}, dimensions={0} | all-to-all | bytes 131072 | tf_op jit(solution)/shard_map/all_to_all | solution.py:172
  105.9 12.2 %psum.7 = bf16[16,128]{1,0:T(8,128)(2,1)S(1)} all-reduce(f32[16,128]{1,0:T(8,128)S(1)} %convert_reduce_fusion), channel_id=1, replica_groups=mesh['zh'=4,'y'=8,'x'=4,'zl'=3,'core'=2] {'zh'}, use_global_device_ids=true, to_apply=%region_1.0 | all-reduce | flops 2048 | bytes 12288 | tf_op jit(solution)/shard_map/psum | solution.py:220
  118.1 13.7 %all_to_all.27 = bf16[24,16,128]{2,1,0:T(8,128)(2,1)S(1)} all-to-all(bf16[24,16,128]{2,1,0:T(8,128)(2,1)S(1)} %broadcast_in_dim.27), channel_id=1, replica_groups=mesh['zh'=4,'y'=8,'x'=4,'zl'=3,'core'=2] {'zl','x','core'}, dimensions={0} | all-to-all | bytes 196608 | tf_op jit(solution)/shard_map/all_to_all | solution.py:172
  131.9 0.7 pad_maximum_fusion.1
  (24 shorter events, 2.3 us)
Async XLA Ops:
  0.6 55.0 %copy-start.4 = (s32[1,1,32,2]{2,3,1,0:T(2,128)S(1)}, s32[1,1,32,2]{2,3,1,0:T(2,128)}, u32[]{:S(2)}) copy-start(s32[1,1,32,2]{2,3,1,0:T(2,128)} %param.11) | copy-start | bytes 772
  0.6 0.8 copy-start.1
  1.4 0.7 copy-start.2
  28.0 32.5 %all-to-all-start.1 = ((bf16[8,4,128,128]{3,2,1,0:T(8,128)(2,1)}), bf16[8,4,128,128]{3,2,1,0:T(8,128)(2,1)S(1)}, u32[]{:S(2)}, u32[]{:S(2)}) async-start(bf16[8,4,128,128]{3,2,1,0:T(8,128)(2,1)} %broadcast_in_dim.10), calls=%async_computation.1 | async-start | bytes 2097152 | tf_op jit(solution)/shard_map/all_to_all | solution.py:172
  36.4 7.1 %collective-permute-start = (bf16[1,128,256]{2,1,0:T(8,128)(2,1)S(1)}, bf16[1,128,256]{2,1,0:T(8,128)(2,1)S(1)}, u32[]{:S(2)}, u32[]{:S(2)}) collective-permute-start(bf16[1,128,256]{2,1,0:T(8,128)(2,1)S(1)} %multiply_convert_fusion), channel_id=1, source_target_pairs={{0,2},{2,4},{4,0},{1,3},{3,5},{5,1},{6,8},{8,10},{10,6},{7,9},{9,1... | collective-permute-start | bytes 196616 | tf_op jit(solution)/shard_map/ppermute | solution.py:184
  39.5 5.6 %collective-permute-start.1 = (bf16[1,128,256]{2,1,0:T(8,128)(2,1)S(1)}, bf16[1,128,256]{2,1,0:T(8,128)(2,1)S(1)}, u32[]{:S(2)}, u32[]{:S(2)}) collective-permute-start(bf16[1,128,256]{2,1,0:T(8,128)(2,1)S(1)} %multiply_convert_fusion), channel_id=1, source_target_pairs={{0,4},{2,0},{4,2},{1,5},{3,1},{5,3},{6,10},{8,6},{10,8},{7,11},{9,... | collective-permute-start | bytes 196616 | tf_op jit(solution)/shard_map/ppermute | solution.py:184
  45.1 10.6 %collective-permute-start.2 = (bf16[3,128,256]{2,1,0:T(8,128)(2,1)S(1)}, bf16[3,128,256]{2,1,0:T(8,128)(2,1)S(1)}, u32[]{:S(2)}, u32[]{:S(2)}) collective-permute-start(bf16[3,128,256]{2,1,0:T(8,128)(2,1)S(1)} %pad_maximum_fusion.refs_0_), channel_id=1, source_target_pairs={{0,6},{6,12},{12,18},{18,0},{1,7},{7,13},{13,19},{19,1},{2,8},{8,1... | collective-permute-start | bytes 589832 | tf_op jit(solution)/shard_map/ppermute | solution.py:184
  48.2 8.1 %collective-permute-start.3 = (bf16[3,128,256]{2,1,0:T(8,128)(2,1)S(1)}, bf16[3,128,256]{2,1,0:T(8,128)(2,1)S(1)}, u32[]{:S(2)}, u32[]{:S(2)}) collective-permute-start(bf16[3,128,256]{2,1,0:T(8,128)(2,1)S(1)} %pad_maximum_fusion.refs_0_), channel_id=1, source_target_pairs={{0,12},{6,18},{12,0},{18,6},{1,13},{7,19},{13,1},{19,7},{2,14},{8,... | collective-permute-start | bytes 589832 | tf_op jit(solution)/shard_map/ppermute | solution.py:184
  52.6 6.6 %collective-permute-start.4 = (bf16[3,128,256]{2,1,0:T(8,128)(2,1)S(1)}, bf16[3,128,256]{2,1,0:T(8,128)(2,1)S(1)}, u32[]{:S(2)}, u32[]{:S(2)}) collective-permute-start(bf16[3,128,256]{2,1,0:T(8,128)(2,1)S(1)} %pad_maximum_fusion.refs_0_), channel_id=1, source_target_pairs={{0,18},{6,0},{12,6},{18,12},{1,19},{7,1},{13,7},{19,13},{2,20},{8,... | collective-permute-start | bytes 589832 | tf_op jit(solution)/shard_map/ppermute | solution.py:184
  60.5 18.4 %copy-start.3 = (s32[1,128]{1,0:T(1,128)S(1)}, s32[1,128]{1,0:T(1,128)}, u32[]{:S(2)}) copy-start(s32[1,128]{1,0:T(1,128)} %param.10) | copy-start | bytes 1540
  60.5 26.7 %copy-start = (bf16[128,256]{1,0:T(8,128)(2,1)S(1)}, bf16[128,256]{1,0:T(8,128)(2,1)}, u32[]{:S(2)}) copy-start(bf16[128,256]{1,0:T(8,128)(2,1)} %weight_ref.1) | copy-start | bytes 196612
  63.4 8.8 %collective-permute-start.5 = (bf16[12,128,128]{2,1,0:T(8,128)(2,1)S(1)}, bf16[12,128,128]{2,1,0:T(8,128)(2,1)S(1)}, u32[]{:S(2)}, u32[]{:S(2)}) collective-permute-start(bf16[12,128,128]{2,1,0:T(8,128)(2,1)S(1)} %get-tuple-element.23), channel_id=1, source_target_pairs={{0,1},{1,0},{2,3},{3,2},{4,5},{5,4},{6,7},{7,6},{8,9},{9,8},{10,11... | collective-permute-start | bytes 1179656 | tf_op jit(solution)/shard_map/ppermute | solution.py:180
  73.9 13.3 %all-to-all-start.2 = ((bf16[12,160,128]{2,1,0:T(8,128)(2,1)}), bf16[12,160,128]{2,1,0:T(8,128)(2,1)S(1)}, u32[]{:S(2)}, u32[]{:S(2)}) async-start(bf16[12,160,128]{2,1,0:T(8,128)(2,1)} %pair_stage.1), calls=%async_computation.2 | async-start | bytes 983040 | tf_op jit(solution)/shard_map/all_to_all | solution.py:172

commit v6 on v5

--- a/solution.py
+++ b/solution.py
@@ -217,7 +217,7 @@
         (Y, CORE, PIECE // CORE, CH),
     ).reshape(Y * CORE, PIECE // CORE, CH)
     piece = jnp.sum(exchange(halves, ("y", "core")).astype(jnp.float32), axis=0)
-    piece = lax.psum(piece, "zh").astype(jnp.bfloat16)
+    piece = lax.psum(piece.astype(jnp.bfloat16), "zh")
     pieces = spread(piece, ("zl", "x", "core"), CORE * ROW_TILES)
     grad = pieces[: CORE * F // PIECE].reshape(F // CH, CH, CH).astype(jnp.float32)
     grad_weight = jnp.concatenate([grad[k] for k in range(F // CH)], axis=1)

time: 133 us -> 133 us (level)
  no operation moved by 1% of the time
where the time goes in v6:
time: 133 us; the launch traced here: 132 us
  blocking collectives  68 us (51%)
  starting transfers between devices  36.1 us (27%)
  waiting for transfers between devices  15.7 us (12%)
  Pallas kernels  5.98 us (4%)
  local copies, waits for them, and re-layouts  2.79 us (2%)
  other arithmetic  2.39 us (2%)
  between operations  1.46 us (1%)
    all_to_all x3, blocking collectives, exchange(): return lax.all_to_all(parts, axes, 0, 0)  56.3 us
    ppermute x5, starting transfers between devices, shifted(): return lax.ppermute(block, axis, [(i, (i + shift) % n) for i in range(n)])  17 us
    all_to_all x2, starting transfers between devices, exchange(): return lax.all_to_all(parts, axes, 0, 0)  12.1 us
    psum x1, blocking collectives, per_device(): piece = lax.psum(piece.astype(jnp.bfloat16), 'zh')  11.6 us
    all_to_all x2, waiting for transfers between devices, exchange(): return lax.all_to_all(parts, axes, 0, 0)  9.48 us
    ppermute x1, starting transfers between devices, swap_cores(): return lax.ppermute(block, 'core', [(0, 1), (1, 0)])  7.05 us
    ppermute x5, waiting for transfers between devices, shifted(): return lax.ppermute(block, axis, [(i, (i + shift) % n) for i in range(n)])  5.01 us
    pallas_call x1, Pallas kernels, tile_product(): pl.pallas_call(tile_kernel, out_shape=(jax.ShapeDtypeStruct((ROW_TILES, N...  3.26 us
  transfers between devices with their start and end apart: 8, of which 6 were waited for; matrix products, arithmetic and copies ran while one was open for 1% of the time, Pallas kernels for 0%

profile of v6, /device:TPU:1, one launch (start us, length us, event | category | flops | bytes accessed | tf_op | source)
XLA Modules:
  0.0 132.4 jit_solution(10129616621119835549)
XLA Ops:
  0.6 0.8 copy-done.1
  2.2 24.6 %all_to_all.25 = bf16[4,128,128]{2,1,0:T(8,128)(2,1)S(1)} all-to-all(bf16[4,128,128]{2,1,0:T(8,128)(2,1)S(1)} %scaled_copies.1), channel_id=1, replica_groups=mesh['zh'=4,'y'=8,'x'=4,'zl'=3,'core'=2] {'zh'}, dimensions={0} | all-to-all | bytes 262144 | tf_op jit(solution)/shard_map/all_to_all | solution.py:172
  26.8 1.2 broadcast_in_dim.10
  28.0 6.8 %all-to-all-start.1 = ((bf16[8,4,128,128]{3,2,1,0:T(8,128)(2,1)}), bf16[8,4,128,128]{3,2,1,0:T(8,128)(2,1)S(1)}, u32[]{:S(2)}, u32[]{:S(2)}) async-start(bf16[8,4,128,128]{3,2,1,0:T(8,128)(2,1)} %broadcast_in_dim.10), calls=%async_computation.1 | async-start | bytes 2097152 | tf_op jit(solution)/shard_map/all_to_all | solution.py:172
  35.5 0.9 multiply_convert_fusion
  36.4 3.1 %collective-permute-start = (bf16[1,128,256]{2,1,0:T(8,128)(2,1)S(1)}, bf16[1,128,256]{2,1,0:T(8,128)(2,1)S(1)}, u32[]{:S(2)}, u32[]{:S(2)}) collective-permute-start(bf16[1,128,256]{2,1,0:T(8,128)(2,1)S(1)} %multiply_convert_fusion), channel_id=1, source_target_pairs={{0,2},{2,4},{4,0},{1,3},{3,5},{5,1},{6,8},{8,10},{10,6},{7,9},{9,1... | collective-permute-start | bytes 196616 | tf_op jit(solution)/shard_map/ppermute | solution.py:184
  39.5 3.4 %collective-permute-start.1 = (bf16[1,128,256]{2,1,0:T(8,128)(2,1)S(1)}, bf16[1,128,256]{2,1,0:T(8,128)(2,1)S(1)}, u32[]{:S(2)}, u32[]{:S(2)}) collective-permute-start(bf16[1,128,256]{2,1,0:T(8,128)(2,1)S(1)} %multiply_convert_fusion), channel_id=1, source_target_pairs={{0,4},{2,0},{4,2},{1,5},{3,1},{5,3},{6,10},{8,6},{10,8},{7,11},{9,... | collective-permute-start | bytes 196616 | tf_op jit(solution)/shard_map/ppermute | solution.py:184
  43.5 1.5 %collective-permute-done.1 = bf16[1,128,256]{2,1,0:T(8,128)(2,1)S(1)} collective-permute-done((bf16[1,128,256]{2,1,0:T(8,128)(2,1)S(1)}, bf16[1,128,256]{2,1,0:T(8,128)(2,1)S(1)}, u32[]{:S(2)}, u32[]{:S(2)}) %collective-permute-start.1) | collective-permute-done | bytes 65568 | tf_op jit(solution)/shard_map/ppermute | solution.py:184
  45.1 3.1 %collective-permute-start.2 = (bf16[3,128,256]{2,1,0:T(8,128)(2,1)S(1)}, bf16[3,128,256]{2,1,0:T(8,128)(2,1)S(1)}, u32[]{:S(2)}, u32[]{:S(2)}) collective-permute-start(bf16[3,128,256]{2,1,0:T(8,128)(2,1)S(1)} %pad_maximum_fusion.refs_0_), channel_id=1, source_target_pairs={{0,6},{6,12},{12,18},{18,0},{1,7},{7,13},{13,19},{19,1},{2,8},{8,1... | collective-permute-start | bytes 589832 | tf_op jit(solution)/shard_map/ppermute | solution.py:184
  48.2 4.4 %collective-permute-start.3 = (bf16[3,128,256]{2,1,0:T(8,128)(2,1)S(1)}, bf16[3,128,256]{2,1,0:T(8,128)(2,1)S(1)}, u32[]{:S(2)}, u32[]{:S(2)}) collective-permute-start(bf16[3,128,256]{2,1,0:T(8,128)(2,1)S(1)} %pad_maximum_fusion.refs_0_), channel_id=1, source_target_pairs={{0,12},{6,18},{12,0},{18,6},{1,13},{7,19},{13,1},{19,7},{2,14},{8,... | collective-permute-start | bytes 589832 | tf_op jit(solution)/shard_map/ppermute | solution.py:184
  52.6 3.1 %collective-permute-start.4 = (bf16[3,128,256]{2,1,0:T(8,128)(2,1)S(1)}, bf16[3,128,256]{2,1,0:T(8,128)(2,1)S(1)}, u32[]{:S(2)}, u32[]{:S(2)}) collective-permute-start(bf16[3,128,256]{2,1,0:T(8,128)(2,1)S(1)} %pad_maximum_fusion.refs_0_), channel_id=1, source_target_pairs={{0,18},{6,0},{12,6},{18,12},{1,19},{7,1},{13,7},{19,13},{2,20},{8,... | collective-permute-start | bytes 589832 | tf_op jit(solution)/shard_map/ppermute | solution.py:184
  56.3 2.9 %collective-permute-done.4.refs_3_ = bf16[3,128,256]{2,1,0:T(8,128)(2,1)S(1)} collective-permute-done((bf16[3,128,256]{2,1,0:T(8,128)(2,1)S(1)}, bf16[3,128,256]{2,1,0:T(8,128)(2,1)S(1)}, u32[]{:S(2)}, u32[]{:S(2)}) %collective-permute-start.4) | collective-permute-done | bytes 196640 | tf_op jit(solution)/shard_map/ppermute | solution.py:184
  59.2 1.3 %all-to-all-done.1.source_ref = bf16[8,4,128,128]{3,2,1,0:T(8,128)(2,1)S(1)} async-done(((bf16[8,4,128,128]{3,2,1,0:T(8,128)(2,1)}), bf16[8,4,128,128]{3,2,1,0:T(8,128)(2,1)S(1)}, u32[]{:S(2)}, u32[]{:S(2)}) %all-to-all-start.1) | async-done | bytes 1048608 | tf_op jit(solution)/shard_map/all_to_all | solution.py:172
  60.5 3.3 %tile_product.1 = (f32[12,128,128]{2,1,0:T(8,128)S(1)}, bf16[12,128,128]{2,1,0:T(8,128)(2,1)S(1)}) custom-call(s32[32]{0:T(128)S(1)} %add_bitcast_fusion.pos_ref, s32[1]{0:T(128)} %bitcast.16.count_ref, s32[1]{0:T(128)} %bitcast.6.core_ref, bf16[32,256,256]{2,1,0:T(8,128)(2,1)} %bitcast.18, bf16[8,4,128,128]{3,2,1,0:T(8,128)(2,1)S(1)} %all-to-all-done.1.source_ref), custom_call_target="tpu_custom_call" | custom-call | flops 536870912 | bytes 8388608 | tf_op jit(solution)/shard_map/tile_product/pallas_call | solution.py:83
  63.8 7.1 %collective-permute-start.5 = (bf16[12,128,128]{2,1,0:T(8,128)(2,1)S(1)}, bf16[12,128,128]{2,1,0:T(8,128)(2,1)S(1)}, u32[]{:S(2)}, u32[]{:S(2)}) collective-permute-start(bf16[12,128,128]{2,1,0:T(8,128)(2,1)S(1)} %get-tuple-element.23), channel_id=1, source_target_pairs={{0,1},{1,0},{2,3},{3,2},{4,5},{5,4},{6,7},{7,6},{8,9},{9,8},{10,11... | collective-permute-start | bytes 1179656 | tf_op jit(solution)/shard_map/ppermute | solution.py:180
  70.9 1.2 collective-permute-done.5.arrived_ref
  72.2 1.8 %pair_stage.1 = bf16[12,160,128]{2,1,0:T(8,128)(2,1)} custom-call(s32[2]{0:T(128)S(1)} %pad_add_fusion.place_ref, f32[12,128,128]{2,1,0:T(8,128)S(1)} %get-tuple-element.22.keep_ref, bf16[12,128,128]{2,1,0:T(8,128)(2,1)S(1)} %collective-permute-done.5.arrived_ref, bf16[3,128,256]{2,1,0:T(8,128)(2,1)S(1)} %pad_maximum_fusion.refs_0_, ...), custom_call_target="tpu_custom_call" | custom-call | flops 100663296 | bytes 3145728 | tf_op jit(solution)/shard_map/pair_stage/pallas_call | solution.py:127
  73.9 5.2 %all-to-all-start.2 = ((bf16[12,160,128]{2,1,0:T(8,128)(2,1)}), bf16[12,160,128]{2,1,0:T(8,128)(2,1)S(1)}, u32[]{:S(2)}, u32[]{:S(2)}) async-start(bf16[12,160,128]{2,1,0:T(8,128)(2,1)} %pair_stage.1), calls=%async_computation.2 | async-start | bytes 983040 | tf_op jit(solution)/shard_map/all_to_all | solution.py:172
  79.3 8.1 %all-to-all-done.2.parts_ref = bf16[12,160,128]{2,1,0:T(8,128)(2,1)S(1)} async-done(((bf16[12,160,128]{2,1,0:T(8,128)(2,1)}), bf16[12,160,128]{2,1,0:T(8,128)(2,1)S(1)}, u32[]{:S(2)}, u32[]{:S(2)}) %all-to-all-start.2) | async-done | bytes 491552 | tf_op jit(solution)/shard_map/all_to_all | solution.py:172
  87.5 0.8 node_stage.1
  88.3 18.0 %all_to_all.26 = bf16[16,16,128]{2,1,0:T(8,128)(2,1)S(1)} all-to-all(bf16[16,16,128]{2,1,0:T(8,128)(2,1)S(1)} %bitcast.19), channel_id=1, replica_groups=mesh['zh'=4,'y'=8,'x'=4,'zl'=3,'core'=2] {'y','core'}, dimensions={0} | all-to-all | bytes 131072 | tf_op jit(solution)/shard_map/all_to_all | solution.py:172
  106.3 11.6 %psum.7 = bf16[16,128]{1,0:T(8,128)(2,1)S(1)} all-reduce(bf16[16,128]{1,0:T(8,128)(2,1)S(1)} %reduce_sum.12), channel_id=1, replica_groups=mesh['zh'=4,'y'=8,'x'=4,'zl'=3,'core'=2] {'zh'}, use_global_device_ids=true, to_apply=%region_1.0 | all-reduce | flops 2048 | bytes 8192 | tf_op jit(solution)/shard_map/psum | solution.py:220
  118.0 13.8 %all_to_all.27 = bf16[24,16,128]{2,1,0:T(8,128)(2,1)S(1)} all-to-all(bf16[24,16,128]{2,1,0:T(8,128)(2,1)S(1)} %broadcast_in_dim.27), channel_id=1, replica_groups=mesh['zh'=4,'y'=8,'x'=4,'zl'=3,'core'=2] {'zl','x','core'}, dimensions={0} | all-to-all | bytes 196608 | tf_op jit(solution)/shard_map/all_to_all | solution.py:172
  131.8 0.7 pad_maximum_fusion.1
  (24 shorter events, 2.3 us)
Async XLA Ops:
  0.6 55.0 %copy-start.4 = (s32[1,1,32,2]{2,3,1,0:T(2,128)S(1)}, s32[1,1,32,2]{2,3,1,0:T(2,128)}, u32[]{:S(2)}) copy-start(s32[1,1,32,2]{2,3,1,0:T(2,128)} %param.11) | copy-start | bytes 772
  0.6 0.8 copy-start.1
  1.4 0.7 copy-start.2
  28.0 32.5 %all-to-all-start.1 = ((bf16[8,4,128,128]{3,2,1,0:T(8,128)(2,1)}), bf16[8,4,128,128]{3,2,1,0:T(8,128)(2,1)S(1)}, u32[]{:S(2)}, u32[]{:S(2)}) async-start(bf16[8,4,128,128]{3,2,1,0:T(8,128)(2,1)} %broadcast_in_dim.10), calls=%async_computation.1 | async-start | bytes 2097152 | tf_op jit(solution)/shard_map/all_to_all | solution.py:172
  36.4 7.1 %collective-permute-start = (bf16[1,128,256]{2,1,0:T(8,128)(2,1)S(1)}, bf16[1,128,256]{2,1,0:T(8,128)(2,1)S(1)}, u32[]{:S(2)}, u32[]{:S(2)}) collective-permute-start(bf16[1,128,256]{2,1,0:T(8,128)(2,1)S(1)} %multiply_convert_fusion), channel_id=1, source_target_pairs={{0,2},{2,4},{4,0},{1,3},{3,5},{5,1},{6,8},{8,10},{10,6},{7,9},{9,1... | collective-permute-start | bytes 196616 | tf_op jit(solution)/shard_map/ppermute | solution.py:184
  39.5 5.6 %collective-permute-start.1 = (bf16[1,128,256]{2,1,0:T(8,128)(2,1)S(1)}, bf16[1,128,256]{2,1,0:T(8,128)(2,1)S(1)}, u32[]{:S(2)}, u32[]{:S(2)}) collective-permute-start(bf16[1,128,256]{2,1,0:T(8,128)(2,1)S(1)} %multiply_convert_fusion), channel_id=1, source_target_pairs={{0,4},{2,0},{4,2},{1,5},{3,1},{5,3},{6,10},{8,6},{10,8},{7,11},{9,... | collective-permute-start | bytes 196616 | tf_op jit(solution)/shard_map/ppermute | solution.py:184
  45.1 10.6 %collective-permute-start.2 = (bf16[3,128,256]{2,1,0:T(8,128)(2,1)S(1)}, bf16[3,128,256]{2,1,0:T(8,128)(2,1)S(1)}, u32[]{:S(2)}, u32[]{:S(2)}) collective-permute-start(bf16[3,128,256]{2,1,0:T(8,128)(2,1)S(1)} %pad_maximum_fusion.refs_0_), channel_id=1, source_target_pairs={{0,6},{6,12},{12,18},{18,0},{1,7},{7,13},{13,19},{19,1},{2,8},{8,1... | collective-permute-start | bytes 589832 | tf_op jit(solution)/shard_map/ppermute | solution.py:184
  48.2 8.1 %collective-permute-start.3 = (bf16[3,128,256]{2,1,0:T(8,128)(2,1)S(1)}, bf16[3,128,256]{2,1,0:T(8,128)(2,1)S(1)}, u32[]{:S(2)}, u32[]{:S(2)}) collective-permute-start(bf16[3,128,256]{2,1,0:T(8,128)(2,1)S(1)} %pad_maximum_fusion.refs_0_), channel_id=1, source_target_pairs={{0,12},{6,18},{12,0},{18,6},{1,13},{7,19},{13,1},{19,7},{2,14},{8,... | collective-permute-start | bytes 589832 | tf_op jit(solution)/shard_map/ppermute | solution.py:184
  52.6 6.6 %collective-permute-start.4 = (bf16[3,128,256]{2,1,0:T(8,128)(2,1)S(1)}, bf16[3,128,256]{2,1,0:T(8,128)(2,1)S(1)}, u32[]{:S(2)}, u32[]{:S(2)}) collective-permute-start(bf16[3,128,256]{2,1,0:T(8,128)(2,1)S(1)} %pad_maximum_fusion.refs_0_), channel_id=1, source_target_pairs={{0,18},{6,0},{12,6},{18,12},{1,19},{7,1},{13,7},{19,13},{2,20},{8,... | collective-permute-start | bytes 589832 | tf_op jit(solution)/shard_map/ppermute | solution.py:184
  60.5 18.7 %copy-start.3 = (s32[1,128]{1,0:T(1,128)S(1)}, s32[1,128]{1,0:T(1,128)}, u32[]{:S(2)}) copy-start(s32[1,128]{1,0:T(1,128)} %param.10) | copy-start | bytes 1540
  60.5 26.9 %copy-start = (bf16[128,256]{1,0:T(8,128)(2,1)S(1)}, bf16[128,256]{1,0:T(8,128)(2,1)}, u32[]{:S(2)}) copy-start(bf16[128,256]{1,0:T(8,128)(2,1)} %weight_ref.1) | copy-start | bytes 196612
  63.8 8.4 %collective-permute-start.5 = (bf16[12,128,128]{2,1,0:T(8,128)(2,1)S(1)}, bf16[12,128,128]{2,1,0:T(8,128)(2,1)S(1)}, u32[]{:S(2)}, u32[]{:S(2)}) collective-permute-start(bf16[12,128,128]{2,1,0:T(8,128)(2,1)S(1)} %get-tuple-element.23), channel_id=1, source_target_pairs={{0,1},{1,0},{2,3},{3,2},{4,5},{5,4},{6,7},{7,6},{8,9},{9,8},{10,11... | collective-permute-start | bytes 1179656 | tf_op jit(solution)/shard_map/ppermute | solution.py:180
  73.9 13.5 %all-to-all-start.2 = ((bf16[12,160,128]{2,1,0:T(8,128)(2,1)}), bf16[12,160,128]{2,1,0:T(8,128)(2,1)S(1)}, u32[]{:S(2)}, u32[]{:S(2)}) async-start(bf16[12,160,128]{2,1,0:T(8,128)(2,1)} %pair_stage.1), calls=%async_computation.2 | async-start | bytes 983040 | tf_op jit(solution)/shard_map/all_to_all | solution.py:172
